TPU v7x, 32 devices: a whole 2x2x4 slice. The times are simulated.
32 devices in a mesh: chan: 4 (over y, x), win: 8 (over z, core).
Axes of the slice: x: 2, y: 2, z: 4, core: 2. Of those that a mesh axis runs over, the one named last changes fastest.
Arguments:
- raw: bfloat16 [32, 3200, 1024], P('win', None, 'chan'), may hold values from -6 to 6
- offsets: int32 [32], P('win'), may hold values from 0 to 128
- quality: int32 [32, 1024], P('win', 'chan'), may hold values 0 or 1
Outputs:
- stack: bfloat16 [384, 2, 1024, 1024], P('win', None, 'chan')
All inputs are finite; a program needn't handle non-finite values. No bound on the sum of `quality` on one device may be relied on, other than what follows from the above.
Results may differ from a plain program's by a relative error of at most 0.0064.
Values may be sent and summed in bfloat16 or wider, within the bound.
No kernel may reach another device: no remote copies, remote signals or barrier semaphores. Data moves between devices by JAX's collectives and lax.ppermute only.
A program may use at most 256 MiB of HBM per device.

v0:
```python
import functools
import math

import jax
import jax.numpy as jnp
import ml_dtypes
import numpy as np
from jax import lax
from jax.experimental import pallas as pl
from jax.experimental.pallas import tpu as pltpu
from jax.sharding import PartitionSpec as P

F = 384
L = 3072
FIRST_BIN = 60
CHUNK_WEIGHTS = (1, 1, 1)
STEP_GROUPS = 2
SPECTRA_MIB = 50

epsilon = 1e-05
MIB = 1024 * 1024


def dft_table():
    sample_idx = np.arange(L, dtype=np.int64)
    bin_idx = FIRST_BIN + np.arange(F, dtype=np.int64)
    residue = bin_idx[:, None] * sample_idx[None, :] % L
    angles = residue.astype(np.float32) * np.float32(2.0 * math.pi / L)
    return np.concatenate([np.cos(angles), -np.sin(angles)], 0).astype(ml_dtypes.bfloat16)


def interleave(windows, bins):
    pair = 16 // (2 * windows)
    out = np.zeros((2 * windows * bins, 2 * windows * bins), np.float32)
    for f in range(bins):
        for p in range(2):
            for w in range(windows):
                row = ((f // pair * 2 + p) * pair + f % pair) * windows + w
                out[row, (w * 2 + p) * bins + f] = 1.0
    return out.astype(ml_dtypes.bfloat16)


def cut(raw_ref, slot, shift_at, window_ref):
    width = raw_ref.shape[2]
    spare = raw_ref.shape[1] - L
    tile = 256
    base = jnp.minimum(shift_at // 16, (spare - 16) // 16) * 16
    rest = shift_at - base
    whole = rest // 8
    fine = rest - whole * 8
    back = jnp.where(fine == 0, 0, 8 - fine)
    keep = lax.broadcasted_iota(jnp.int32, (tile // 8, 8, width), 1) < 8 - fine
    count = tile // 8
    for step in range(L // tile):
        start = pl.multiple_of(base + step * tile, 16)
        rows = raw_ref[slot, pl.ds(start, tile + 16), :].astype(jnp.float32).reshape(count + 2, 8, width)
        rolled = pltpu.roll(rows, back, 1)
        upper = jnp.where(whole == 0, rolled[1 : count + 1], rolled[2:])
        lower = jnp.where(whole == 0, rolled[:count], jnp.where(whole == 1, rolled[1 : count + 1], rolled[2:]))
        moved = jnp.where(keep, lower, upper)
        window_ref[step * tile : (step + 1) * tile, :] = moved.reshape(tile, width).astype(jnp.bfloat16)


def spectra_kernel(offsets_ref, table_hbm, mix_hbm, raw_hbm, quality_hbm, keep_ref, give_ref, *scratch):
    table_ref, mix_ref, quality_ref, raw_ref, white, mixed, sems = scratch[:7]
    cuts = scratch[7:]
    windows, _, width = raw_ref.shape
    loads = [pltpu.make_async_copy(raw_hbm.at[w], raw_ref.at[w], sems.at[w]) for w in range(windows)]
    table_load = pltpu.make_async_copy(table_hbm, table_ref, sems.at[windows])
    mix_load = pltpu.make_async_copy(mix_hbm, mix_ref, sems.at[windows + 1])
    quality_load = pltpu.make_async_copy(quality_hbm, quality_ref, sems.at[windows + 2])
    for load in (loads[0], table_load, *loads[1:], quality_load, mix_load):
        load.start()
    loads[0].wait()
    cut(raw_ref, 0, offsets_ref[0], cuts[0])
    for load in (table_load, *loads[1:], quality_load, mix_load):
        load.wait()
    for w in range(windows):
        if w + 1 < windows:
            cut(raw_ref, w + 1, offsets_ref[w + 1], cuts[w + 1])
        transform = jnp.dot(table_ref[...], cuts[w][...], preferred_element_type=jnp.float32)
        band_power = jnp.sum(transform * transform, axis=0, keepdims=True) / F
        usable = quality_ref[w : w + 1, :].astype(jnp.float32)
        white[w] = (transform * (lax.rsqrt(band_power + epsilon) * usable)).astype(jnp.bfloat16)

    pair = 16 // (2 * windows)
    bins = mix_ref.shape[0] // (2 * windows)
    groups = bins // pair
    for block in range(F // bins):
        parts = [
            white[v, p * F + block * bins : p * F + (block + 1) * bins, :] for v in range(windows) for p in range(2)
        ]
        product = jnp.dot(mix_ref[...], jnp.concatenate(parts, 0), preferred_element_type=jnp.float32)
        mixed[block * groups : (block + 1) * groups] = product.astype(jnp.bfloat16).reshape(groups, 16, width)
    me = lax.axis_index("win")
    chip, core = me // 2, me % 2
    chips, share = keep_ref.shape[:2]
    for k in range(chips):
        at = (chip ^ k) * 2 * share
        keep_ref[k] = mixed[pl.ds(at + core * share, share)]
        give_ref[k] = mixed[pl.ds(at + (1 - core) * share, share)]


def in_vmem(count):
    return [pl.BlockSpec(memory_space=pltpu.VMEM)] * count


def spectra(raw, offsets, quality, table, mix, dests):
    windows, _, width = raw.shape
    groups = F * 2 * windows // 16
    blocks = (dests // 2, groups // dests, 16, width)
    return pl.pallas_call(
        spectra_kernel,
        in_specs=[pl.BlockSpec(memory_space=pltpu.SMEM)] + [pl.BlockSpec(memory_space=pl.ANY)] * 4,
        out_specs=in_vmem(2),
        scratch_shapes=[
            pltpu.VMEM(table.shape, table.dtype),
            pltpu.VMEM(mix.shape, mix.dtype),
            pltpu.VMEM(quality.shape, quality.dtype),
            pltpu.VMEM(raw.shape, raw.dtype),
            pltpu.VMEM((windows, 2 * F, width), jnp.bfloat16),
            pltpu.VMEM((groups, 16, width), jnp.bfloat16),
            pltpu.SemaphoreType.DMA((windows + 3,)),
            *[pltpu.VMEM((L, width), jnp.bfloat16)] * windows,
        ],
        out_shape=[jax.ShapeDtypeStruct(blocks, jnp.bfloat16)] * 2,
        compiler_params=pltpu.CompilerParams(vmem_limit_bytes=SPECTRA_MIB * MIB),
        cost_estimate=pl.CostEstimate(
            flops=2 * windows * 2 * F * L * width, bytes_accessed=2 * windows * raw.shape[1] * width + 4 * F * L, transcendentals=0
        ),
        name="spectra",
    )(offsets, table, mix, raw, quality)


def join_kernel(moves, *refs):
    out_ref = refs[-1]
    groups = out_ref.shape[1]
    to = 0
    for i, at, source, count in moves:
        out_ref[to : to + count] = refs[i][source : source + count, at : at + groups]
        to += count


def join(views, groups):
    arrays, moves = [], []
    for x, *where in views:
        known = [i for i, y in enumerate(arrays) if y is x]
        if not known:
            arrays.append(x)
        moves.append((known[0] if known else len(arrays) - 1, *where))
    shape = (sum(move[3] for move in moves), groups, *arrays[0].shape[2:])
    return pl.pallas_call(
        functools.partial(join_kernel, moves),
        in_specs=in_vmem(len(arrays)),
        out_specs=in_vmem(1)[0],
        out_shape=jax.ShapeDtypeStruct(shape, arrays[0].dtype),
        compiler_params=pltpu.CompilerParams(vmem_limit_bytes=12 * MIB),
        cost_estimate=pl.CostEstimate(flops=0, bytes_accessed=4 * math.prod(shape), transcendentals=0),
        name="join",
    )(*arrays)


def view(ref, group, at, sources):
    return ref[sources[0] : sources[1], group - at].reshape(-1, ref.shape[-1])


def turn_kernel(first_group, views, *refs):
    out_ref = refs[-1]
    _, _, width, depth = out_ref.shape

    def body(g, carry):
        x = jnp.concatenate([view(refs[i], first_group + g, *where) for i, where in enumerate(views)], 0)
        by_part = x.astype(jnp.float32).reshape(depth // 16, 16, width)
        turned = jnp.concatenate([by_part[:, 8:], -by_part[:, :8]], 1)
        out_ref[g, 0] = by_part.reshape(depth, width).T.astype(jnp.bfloat16)
        out_ref[g, 1] = turned.reshape(depth, width).T.astype(jnp.bfloat16)
        return carry

    lax.fori_loop(0, out_ref.shape[0], body, 0)


def turn(items, first_group, groups):
    rows, width = items[0][0].shape[2:]
    depth = sum(sources[1] - sources[0] for _, _, sources in items) * rows
    return pl.pallas_call(
        functools.partial(turn_kernel, first_group, [item[1:] for item in items]),
        in_specs=in_vmem(len(items)),
        out_specs=in_vmem(1)[0],
        out_shape=jax.ShapeDtypeStruct((groups, 2, width, depth), jnp.bfloat16),
        compiler_params=pltpu.CompilerParams(vmem_limit_bytes=12 * MIB),
        cost_estimate=pl.CostEstimate(flops=0, bytes_accessed=8 * groups * width * depth, transcendentals=0),
        name="turn",
    )(*[item[0] for item in items])


def closed_walk(i, members):
    return jnp.where(i < members // 2, i, members - 1 - i + members // 2)


def stack_kernel(windows, scale, first_group, layout, left_ref, *refs):
    out_ref = refs[-1]
    pair = 16 // (2 * windows)
    width, depth = left_ref.shape[2:]
    step_groups = out_ref.shape[0] // pair
    members = len(layout)
    where = closed_walk(lax.axis_index("chan"), members)
    bin_of = lax.broadcasted_iota(jnp.int32, (width, depth), 1) % 8 // windows
    masks = [jnp.where(bin_of == b, 1.0, 0.0).astype(jnp.bfloat16) for b in range(pair)]
    for s in range(step_groups):
        g = pl.program_id(0) * step_groups + s
        sides = [left_ref[g, part] for part in range(2)]
        for step, items in layout:
            right = jnp.concatenate([view(refs[i], first_group + g, *item) for i, item in items], 0)
            column = closed_walk(lax.rem(where + (step + members), members), members)
            columns = pl.ds(pl.multiple_of(column * width, width), width)
            for b in range(pair):
                for part in range(2):
                    product = jnp.dot(sides[part] * masks[b], right, preferred_element_type=jnp.float32)
                    out_ref[s * pair + b, part, :, columns] = (product * scale).astype(jnp.bfloat16)


def stack(left, steps, into, first_group, bins, windows, sources):
    members = len(steps)
    groups, _, width, depth = left.shape
    pair = 16 // (2 * windows)
    step_groups = max(n for n in range(1, STEP_GROUPS + 1) if groups % n == 0 and first_group % n == 0)
    operands, layout = [left], []
    for step, items in steps:
        layout.append((step, [(len(operands) - 1 + i, item[1:]) for i, item in enumerate(items)]))
        operands += [item[0] for item in items]
    in_specs = in_vmem(len(operands))
    aliases = {}
    if into is not None:
        aliases = {len(operands): 0}
        operands.append(into)
        in_specs.append(pl.BlockSpec(memory_space=pl.ANY))
    block = (step_groups * pair, 2, width, members * width)
    return pl.pallas_call(
        functools.partial(stack_kernel, windows, 1.0 / math.sqrt(sources), first_group, layout),
        grid=(groups // step_groups,),
        in_specs=in_specs,
        out_specs=pl.BlockSpec(block, lambda g: (first_group // step_groups + g, 0, 0, 0)),
        out_shape=jax.ShapeDtypeStruct((bins, 2, width, members * width), jnp.bfloat16),
        input_output_aliases=aliases,
        compiler_params=pltpu.CompilerParams(vmem_limit_bytes=24 * MIB, dimension_semantics=("arbitrary",)),
        cost_estimate=pl.CostEstimate(
            flops=4 * groups * pair * depth * width * width * members,
            bytes_accessed=4 * groups * pair * width * members * width,
            transcendentals=0,
        ),
        name="stack",
    )(*operands)


def after(arrays, *earlier):
    return list(lax.optimization_barrier((tuple(arrays), earlier))[0])


def ring_walk(members):
    ring = [i if i < members // 2 else members - 1 - i + members // 2 for i in range(members)]
    return [(ring[i], ring[(i + 1) % members]) for i in range(members)]


def ring_start(x, members):
    ahead = ring_walk(members)
    back = [(b, a) for a, b in ahead]
    left = right = x
    blocks = [(0, [x])]
    for step in range(1, (members + 1) // 2):
        left = lax.ppermute(left, "chan", ahead)
        right = lax.ppermute(right, "chan", back)
        blocks += [(-step, [left]), (step, [right])]
    return blocks


def ring_finish(blocks, members, *earlier):
    if members % 2:
        return blocks
    ahead = ring_walk(members)
    left, right = blocks[-2][1][0], blocks[-1][1][0]
    if earlier:
        left, right = after((left, right), *earlier)
    cut_at = left.shape[0] // 2
    first = lax.ppermute(left[:cut_at], "chan", ahead)
    second = lax.ppermute(right[cut_at:], "chan", [(b, a) for a, b in ahead])
    return blocks + [(members // 2, [first, second])]


def neighbours(blocks):
    return [array for step, arrays in blocks if step for array in arrays]


def chunk_starts(share):
    total, starts, seen = sum(CHUNK_WEIGHTS), [0], 0
    for weight in CHUNK_WEIGHTS:
        seen += weight
        starts.append(round(share * seen / total))
    return starts


def local(dests, members, raw, offsets, quality):
    windows = raw.shape[0]
    pair = 16 // (2 * windows)
    bins = F // dests
    share = bins // pair
    chips = dests // 2
    assert chips & (chips - 1) == 0
    starts = chunk_starts(share)
    chunks = list(zip(starts[:-1], starts[1:]))
    table = jnp.asarray(dft_table())
    mix = jnp.asarray(interleave(windows, 256 // (2 * windows)))

    keep, give = spectra(raw, offsets, quality, table, mix, dests)
    other = lax.ppermute(give, "win", [(i, i ^ 1) for i in range(dests)])
    own = join([(keep, 0, 0, 1), (other, 0, 0, 1)], share)
    own_start = ring_start(own, members)
    own_blocks = ring_finish(own_start, members)

    pieces = []
    for start, stop in chunks:
        came = []
        for k in range(1, chips):
            sent = join([(keep, start, k, 1), (other, start, k, 1)], stop - start)
            if pieces:
                sent = after([sent], *neighbours(own_start), pieces[-1][0])[0]
            came.append(lax.ppermute(sent, "win", [(i, i ^ (2 * k)) for i in range(dests)]))
        pieces.append(came)

    out = None
    for n, ((start, stop), came) in enumerate(zip(chunks, pieces)):
        far = join([(x, 0, 0, 2) for x in came], stop - start)
        begun = ring_start(far, members)
        blocks = ring_finish(begun, members, *([] if out is None else [out]))
        steps = []
        for (step, own_arrays), (_, arrays) in zip(own_blocks, blocks):
            views = [(x, 0, (0, x.shape[0])) for x in own_arrays] + [(x, start, (0, x.shape[0])) for x in arrays]
            steps.append((step, views))
        left = turn(steps[0][1], start, stop - start)
        out = stack(left, steps, out, start, bins, windows, dests * windows)
    return out


def solution(mesh):
    in_specs = (P("win", None, "chan"), P("win"), P("win", "chan"))
    out_specs = P("win", None, "chan", None)
    run = functools.partial(local, mesh.shape["win"], mesh.shape["chan"])
    return jax.shard_map(run, mesh=mesh, in_specs=in_specs, out_specs=out_specs, check_vma=False)
```

profile of v0, /device:TPU:0, one launch (start us, length us, event | category | flops | bytes accessed | tf_op | source)
XLA Modules:
  0.0 96.6 jit_solution(5755228093131547186)
XLA Ops:
  0.0 0.0 copy-start
  0.0 0.7 copy-done
  0.7 0.0 copy-start.1
  0.7 0.7 copy-done.1
  1.3 0.9 copy-done.2
  2.2 10.8 %spectra.1 = (bf16[4,24,16,256]{3,2,1,0:T(8,128)(2,1)S(1)}, bf16[4,24,16,256]{3,2,1,0:T(8,128)(2,1)S(1)}) custom-call(s32[4]{0:T(128)S(1)} %copy-done.1, bf16[768,3072]{1,0:T(8,128)(2,1)} %constant.4.clone.table_hbm, bf16[256,256]{1,0:T(8,128)(2,1)S(1)} %copy-done.2, bf16[4,3200,256]{2,1,0:T(8,128)(2,1)} %raw_hbm.1, s32[4,256]{1,0:T(4,128)S(1)} %copy-done), custom_call_target="tpu_custom_call" | custom-call | flops 4831838208 | bytes 11272192 | tf_op jit(solution)/shard_map/spectra/pallas_call | solution.py:112
  13.0 0.5 collective-permute-start
  13.6 1.9 %collective-permute-done.refs_1_ = bf16[4,24,16,256]{3,2,1,0:T(8,128)(2,1)S(1)} collective-permute-done((bf16[4,24,16,256]{3,2,1,0:T(8,128)(2,1)S(1)}, bf16[4,24,16,256]{3,2,1,0:T(8,128)(2,1)S(1)}, u32[]{:S(2)}, u32[]{:S(2)}) %collective-permute-start) | collective-permute-done | bytes 786464 | tf_op jit(solution)/shard_map/ppermute | solution.py:314
  15.5 3.0 %collective-permute-start.3 = (bf16[2,8,16,256]{3,2,1,0:T(8,128)(2,1)S(1)}, bf16[2,8,16,256]{3,2,1,0:T(8,128)(2,1)S(1)}, u32[]{:S(2)}, u32[]{:S(2)}) collective-permute-start(bf16[2,8,16,256]{3,2,1,0:T(8,128)(2,1)S(1)} %join.16), channel_id=1, source_target_pairs={{0,2},{1,3},{2,0},{3,1},{4,6},{5,7},{6,4},{7,5},{8,10},{9,11},{10,... | collective-permute-start | bytes 393224 | tf_op jit(solution)/shard_map/ppermute | solution.py:326
  18.5 2.7 %collective-permute-start.16 = (bf16[2,8,16,256]{3,2,1,0:T(8,128)(2,1)S(1)}, bf16[2,8,16,256]{3,2,1,0:T(8,128)(2,1)S(1)}, u32[]{:S(2)}, u32[]{:S(2)}) collective-permute-start(bf16[2,8,16,256]{3,2,1,0:T(8,128)(2,1)S(1)} %join.23), channel_id=1, source_target_pairs={{0,4},{1,5},{2,6},{3,7},{4,0},{5,1},{6,2},{7,3},{8,12},{9,13},{10,... | collective-permute-start | bytes 393224 | tf_op jit(solution)/shard_map/ppermute | solution.py:326
  21.2 0.1 collective-permute-start.17
  21.3 1.7 %collective-permute-start.1 = (bf16[2,24,16,256]{3,2,1,0:T(8,128)(2,1)S(1)}, bf16[2,24,16,256]{3,2,1,0:T(8,128)(2,1)S(1)}, u32[]{:S(2)}, u32[]{:S(2)}) collective-permute-start(bf16[2,24,16,256]{3,2,1,0:T(8,128)(2,1)S(1)} %join.13.refs_0_), channel_id=1, source_target_pairs={{0,8},{8,24},{24,16},{16,0},{1,9},{9,25},{25,17},{17,1},{2,10},{10... | collective-permute-start | bytes 1179656 | tf_op jit(solution)/shard_map/ppermute | solution.py:270
  23.0 0.3 collective-permute-start.2
  23.4 0.8 collective-permute-done.3.refs_0_
  24.1 7.3 %collective-permute-done.16.refs_1_ = bf16[2,8,16,256]{3,2,1,0:T(8,128)(2,1)S(1)} collective-permute-done((bf16[2,8,16,256]{3,2,1,0:T(8,128)(2,1)S(1)}, bf16[2,8,16,256]{3,2,1,0:T(8,128)(2,1)S(1)}, u32[]{:S(2)}, u32[]{:S(2)}) %collective-permute-start.16) | collective-permute-done | bytes 131104 | tf_op jit(solution)/shard_map/ppermute | solution.py:326
  31.5 0.0 collective-permute-done.17.refs_2_
  31.5 1.5 %collective-permute-start.18 = (bf16[6,8,16,256]{3,2,1,0:T(8,128)(2,1)S(1)}, bf16[6,8,16,256]{3,2,1,0:T(8,128)(2,1)S(1)}, u32[]{:S(2)}, u32[]{:S(2)}) collective-permute-start(bf16[6,8,16,256]{3,2,1,0:T(8,128)(2,1)S(1)} %join.25.refs_1_), channel_id=1, source_target_pairs={{0,8},{8,24},{24,16},{16,0},{1,9},{9,25},{25,17},{17,1},{2,10},{10... | collective-permute-start | bytes 1179656 | tf_op jit(solution)/shard_map/ppermute | solution.py:270
  33.1 0.5 collective-permute-start.19
  33.6 0.0 collective-permute-done.1.refs_2_
  33.6 1.5 %collective-permute-start.10 = (bf16[1,24,16,256]{3,2,1,0:T(8,128)(2,1)S(1)}, bf16[1,24,16,256]{3,2,1,0:T(8,128)(2,1)S(1)}, u32[]{:S(2)}, u32[]{:S(2)}) collective-permute-start(bf16[1,24,16,256]{3,2,1,0:T(8,128)(2,1)S(1)} %slice.32), channel_id=1, source_target_pairs={{0,8},{8,24},{24,16},{16,0},{1,9},{9,25},{25,17},{17,1},{2,10},{10... | collective-permute-start | bytes 589832 | tf_op jit(solution)/shard_map/ppermute | solution.py:284
  35.2 0.0 collective-permute-done.2.refs_4_
  35.2 2.7 %collective-permute-start.13 = (bf16[2,8,16,256]{3,2,1,0:T(8,128)(2,1)S(1)}, bf16[2,8,16,256]{3,2,1,0:T(8,128)(2,1)S(1)}, u32[]{:S(2)}, u32[]{:S(2)}) collective-permute-start(bf16[2,8,16,256]{3,2,1,0:T(8,128)(2,1)S(1)} %join.21), channel_id=1, source_target_pairs={{0,6},{1,7},{2,4},{3,5},{4,2},{5,3},{6,0},{7,1},{8,14},{9,15},{10,... | collective-permute-start | bytes 393224 | tf_op jit(solution)/shard_map/ppermute | solution.py:326
  37.9 1.1 %collective-permute-start.12 = (bf16[2,8,16,256]{3,2,1,0:T(8,128)(2,1)S(1)}, bf16[2,8,16,256]{3,2,1,0:T(8,128)(2,1)S(1)}, u32[]{:S(2)}, u32[]{:S(2)}) collective-permute-start(bf16[2,8,16,256]{3,2,1,0:T(8,128)(2,1)S(1)} %join.20), channel_id=1, source_target_pairs={{0,4},{1,5},{2,6},{3,7},{4,0},{5,1},{6,2},{7,3},{8,12},{9,13},{10,... | collective-permute-start | bytes 393224 | tf_op jit(solution)/shard_map/ppermute | solution.py:326
  39.0 3.6 %collective-permute-done.18.refs_3_ = bf16[6,8,16,256]{3,2,1,0:T(8,128)(2,1)S(1)} collective-permute-done((bf16[6,8,16,256]{3,2,1,0:T(8,128)(2,1)S(1)}, bf16[6,8,16,256]{3,2,1,0:T(8,128)(2,1)S(1)}, u32[]{:S(2)}, u32[]{:S(2)}) %collective-permute-start.18) | collective-permute-done | bytes 393248 | tf_op jit(solution)/shard_map/ppermute | solution.py:270
  42.7 3.2 %collective-permute-start.4 = (bf16[2,8,16,256]{3,2,1,0:T(8,128)(2,1)S(1)}, bf16[2,8,16,256]{3,2,1,0:T(8,128)(2,1)S(1)}, u32[]{:S(2)}, u32[]{:S(2)}) collective-permute-start(bf16[2,8,16,256]{3,2,1,0:T(8,128)(2,1)S(1)} %join.15), channel_id=1, source_target_pairs={{0,2},{1,3},{2,0},{3,1},{4,6},{5,7},{6,4},{7,5},{8,10},{9,11},{10,... | collective-permute-start | bytes 393224 | tf_op jit(solution)/shard_map/ppermute | solution.py:326
  45.9 0.0 collective-permute-done.19.refs_5_
  45.9 1.6 %collective-permute-start.11 = (bf16[1,24,16,256]{3,2,1,0:T(8,128)(2,1)S(1)}, bf16[1,24,16,256]{3,2,1,0:T(8,128)(2,1)S(1)}, u32[]{:S(2)}, u32[]{:S(2)}) collective-permute-start(bf16[1,24,16,256]{3,2,1,0:T(8,128)(2,1)S(1)} %slice.33), channel_id=1, source_target_pairs={{8,0},{24,8},{16,24},{0,16},{9,1},{25,9},{17,25},{1,17},{10,2},{26... | collective-permute-start | bytes 589832 | tf_op jit(solution)/shard_map/ppermute | solution.py:285
  47.5 0.0 collective-permute-done.13.refs_2_
  47.5 0.6 collective-permute-start.20
  48.1 0.0 collective-permute-done.12.refs_1_
  48.1 1.6 %collective-permute-start.21 = (bf16[3,8,16,256]{3,2,1,0:T(8,128)(2,1)S(1)}, bf16[3,8,16,256]{3,2,1,0:T(8,128)(2,1)S(1)}, u32[]{:S(2)}, u32[]{:S(2)}) collective-permute-start(bf16[3,8,16,256]{3,2,1,0:T(8,128)(2,1)S(1)} %slice.35), channel_id=1, source_target_pairs={{8,0},{24,8},{16,24},{0,16},{9,1},{25,9},{17,25},{1,17},{10,2},{26... | collective-permute-start | bytes 589832 | tf_op jit(solution)/shard_map/ppermute | solution.py:285
  49.7 0.0 collective-permute-done.4.refs_0_
  49.7 1.3 %collective-permute-start.14 = (bf16[6,8,16,256]{3,2,1,0:T(8,128)(2,1)S(1)}, bf16[6,8,16,256]{3,2,1,0:T(8,128)(2,1)S(1)}, u32[]{:S(2)}, u32[]{:S(2)}) collective-permute-start(bf16[6,8,16,256]{3,2,1,0:T(8,128)(2,1)S(1)} %join.22.refs_1_), channel_id=1, source_target_pairs={{0,8},{8,24},{24,16},{16,0},{1,9},{9,25},{25,17},{17,1},{2,10},{10... | collective-permute-start | bytes 1179656 | tf_op jit(solution)/shard_map/ppermute | solution.py:270
  51.0 0.0 collective-permute-done.10.refs_6_
  51.0 0.8 collective-permute-start.15
  51.9 0.8 turn.5.left_ref
  52.7 1.1 %collective-permute-done.11.refs_7_ = bf16[1,24,16,256]{3,2,1,0:T(8,128)(2,1)S(1)} collective-permute-done((bf16[1,24,16,256]{3,2,1,0:T(8,128)(2,1)S(1)}, bf16[1,24,16,256]{3,2,1,0:T(8,128)(2,1)S(1)}, u32[]{:S(2)}, u32[]{:S(2)}) %collective-permute-start.11) | collective-permute-done | bytes 196640 | tf_op jit(solution)/shard_map/ppermute | solution.py:285
  53.8 1.6 %collective-permute-start.7 = (bf16[2,8,16,256]{3,2,1,0:T(8,128)(2,1)S(1)}, bf16[2,8,16,256]{3,2,1,0:T(8,128)(2,1)S(1)}, u32[]{:S(2)}, u32[]{:S(2)}) collective-permute-start(bf16[2,8,16,256]{3,2,1,0:T(8,128)(2,1)S(1)} %join.18), channel_id=1, source_target_pairs={{0,6},{1,7},{2,4},{3,5},{4,2},{5,3},{6,0},{7,1},{8,14},{9,15},{10,... | collective-permute-start | bytes 393224 | tf_op jit(solution)/shard_map/ppermute | solution.py:326
  55.4 0.0 collective-permute-done.20.refs_8_
  55.4 1.1 %collective-permute-start.6 = (bf16[2,8,16,256]{3,2,1,0:T(8,128)(2,1)S(1)}, bf16[2,8,16,256]{3,2,1,0:T(8,128)(2,1)S(1)}, u32[]{:S(2)}, u32[]{:S(2)}) collective-permute-start(bf16[2,8,16,256]{3,2,1,0:T(8,128)(2,1)S(1)} %join.17), channel_id=1, source_target_pairs={{0,4},{1,5},{2,6},{3,7},{4,0},{5,1},{6,2},{7,3},{8,12},{9,13},{10,... | collective-permute-start | bytes 393224 | tf_op jit(solution)/shard_map/ppermute | solution.py:326
  56.5 1.5 %collective-permute-done.21.refs_9_ = bf16[3,8,16,256]{3,2,1,0:T(8,128)(2,1)S(1)} collective-permute-done((bf16[3,8,16,256]{3,2,1,0:T(8,128)(2,1)S(1)}, bf16[3,8,16,256]{3,2,1,0:T(8,128)(2,1)S(1)}, u32[]{:S(2)}, u32[]{:S(2)}) %collective-permute-start.21) | collective-permute-done | bytes 196640 | tf_op jit(solution)/shard_map/ppermute | solution.py:285
  58.0 0.3 collective-permute-start.5
  58.3 7.9 %stack.3.refs_10_ = bf16[48,2,256,1024]{3,2,1,0:T(8,128)(2,1)} custom-call(bf16[8,2,256,128]{3,2,1,0:T(8,128)(2,1)S(1)} %turn.5.left_ref, bf16[2,24,16,256]{3,2,1,0:T(8,128)(2,1)S(1)} %join.13.refs_0_, bf16[6,8,16,256]{3,2,1,0:T(8,128)(2,1)S(1)} %join.25.refs_1_, bf16[2,24,16,256]{3,2,1,0:T(8,128)(2,1)S(1)} %collective-permute-done.1.refs_2_, ...), custom_call_target="tpu_custom_call" | custom-call | flops 2147483648 | bytes 16777216 | tf_op jit(solution)/shard_map/stack/pallas_call | solution.py:238
  66.2 0.0 collective-permute-done.14.refs_3_
  66.2 0.0 collective-permute-done.15.refs_5_
  66.2 1.4 %collective-permute-start.22 = (bf16[3,8,16,256]{3,2,1,0:T(8,128)(2,1)S(1)}, bf16[3,8,16,256]{3,2,1,0:T(8,128)(2,1)S(1)}, u32[]{:S(2)}, u32[]{:S(2)}) collective-permute-start(bf16[3,8,16,256]{3,2,1,0:T(8,128)(2,1)S(1)} %slice.28), channel_id=1, source_target_pairs={{0,8},{8,24},{24,16},{16,0},{1,9},{9,25},{25,17},{17,1},{2,10},{10... | collective-permute-start | bytes 589832 | tf_op jit(solution)/shard_map/ppermute | solution.py:284
  67.7 0.7 collective-permute-start.23
  68.4 0.0 collective-permute-done.7.refs_2_
  68.4 0.0 collective-permute-done.6.refs_1_
  68.4 0.0 collective-permute-done.5.refs_0_
  68.4 1.4 %collective-permute-start.8 = (bf16[6,8,16,256]{3,2,1,0:T(8,128)(2,1)S(1)}, bf16[6,8,16,256]{3,2,1,0:T(8,128)(2,1)S(1)}, u32[]{:S(2)}, u32[]{:S(2)}) collective-permute-start(bf16[6,8,16,256]{3,2,1,0:T(8,128)(2,1)S(1)} %join.19.refs_1_), channel_id=1, source_target_pairs={{0,8},{8,24},{24,16},{16,0},{1,9},{9,25},{25,17},{17,1},{2,10},{10... | collective-permute-start | bytes 1179656 | tf_op jit(solution)/shard_map/ppermute | solution.py:270
  69.8 0.7 collective-permute-start.9
  70.5 0.8 turn.4.left_ref
  71.4 1.7 %collective-permute-done.22.refs_8_ = bf16[3,8,16,256]{3,2,1,0:T(8,128)(2,1)S(1)} collective-permute-done((bf16[3,8,16,256]{3,2,1,0:T(8,128)(2,1)S(1)}, bf16[3,8,16,256]{3,2,1,0:T(8,128)(2,1)S(1)}, u32[]{:S(2)}, u32[]{:S(2)}) %collective-permute-start.22) | collective-permute-done | bytes 196640 | tf_op jit(solution)/shard_map/ppermute | solution.py:284
  73.1 1.3 %collective-permute-done.23.refs_9_ = bf16[3,8,16,256]{3,2,1,0:T(8,128)(2,1)S(1)} collective-permute-done((bf16[3,8,16,256]{3,2,1,0:T(8,128)(2,1)S(1)}, bf16[3,8,16,256]{3,2,1,0:T(8,128)(2,1)S(1)}, u32[]{:S(2)}, u32[]{:S(2)}) %collective-permute-start.23) | collective-permute-done | bytes 196640 | tf_op jit(solution)/shard_map/ppermute | solution.py:285
  74.4 7.9 %stack.4.refs_10_ = bf16[48,2,256,1024]{3,2,1,0:T(8,128)(2,1)} custom-call(bf16[8,2,256,128]{3,2,1,0:T(8,128)(2,1)S(1)} %turn.4.left_ref, bf16[2,24,16,256]{3,2,1,0:T(8,128)(2,1)S(1)} %join.13.refs_0_, bf16[6,8,16,256]{3,2,1,0:T(8,128)(2,1)S(1)} %join.22.refs_1_, ...), custom_call_target="tpu_custom_call", output_to_operand_aliasing={{}: (11, {})} | custom-call | flops 2147483648 | bytes 16777216 | tf_op jit(solution)/shard_map/stack/pallas_call | solution.py:238
  82.3 0.0 collective-permute-done.8.refs_3_
  82.3 0.0 collective-permute-done.9.refs_5_
  82.3 0.7 collective-permute-start.24
  83.0 1.5 %collective-permute-start.25 = (bf16[3,8,16,256]{3,2,1,0:T(8,128)(2,1)S(1)}, bf16[3,8,16,256]{3,2,1,0:T(8,128)(2,1)S(1)}, u32[]{:S(2)}, u32[]{:S(2)}) collective-permute-start(bf16[3,8,16,256]{3,2,1,0:T(8,128)(2,1)S(1)} %slice.31), channel_id=1, source_target_pairs={{8,0},{24,8},{16,24},{0,16},{9,1},{25,9},{17,25},{1,17},{10,2},{26... | collective-permute-start | bytes 589832 | tf_op jit(solution)/shard_map/ppermute | solution.py:285
  84.4 0.8 turn.3.left_ref
  85.3 2.7 %collective-permute-done.24.refs_8_ = bf16[3,8,16,256]{3,2,1,0:T(8,128)(2,1)S(1)} collective-permute-done((bf16[3,8,16,256]{3,2,1,0:T(8,128)(2,1)S(1)}, bf16[3,8,16,256]{3,2,1,0:T(8,128)(2,1)S(1)}, u32[]{:S(2)}, u32[]{:S(2)}) %collective-permute-start.24) | collective-permute-done | bytes 196640 | tf_op jit(solution)/shard_map/ppermute | solution.py:284
  88.0 0.7 collective-permute-done.25.refs_9_
  88.7 7.9 %stack.5 = bf16[48,2,256,1024]{3,2,1,0:T(8,128)(2,1)} custom-call(bf16[8,2,256,128]{3,2,1,0:T(8,128)(2,1)S(1)} %turn.3.left_ref, bf16[2,24,16,256]{3,2,1,0:T(8,128)(2,1)S(1)} %join.13.refs_0_, bf16[6,8,16,256]{3,2,1,0:T(8,128)(2,1)S(1)} %join.19.refs_1_, ...), custom_call_target="tpu_custom_call", output_to_operand_aliasing={{}: (11, {})} | custom-call | flops 2147483648 | bytes 16777216 | tf_op jit(solution)/shard_map/stack/pallas_call | solution.py:238
  (22 shorter events, 0.3 us)
Async XLA Ops:
  0.0 0.7 copy-start
  0.7 0.7 copy-start.1
  1.3 0.9 copy-start.2
  13.0 2.4 %collective-permute-start = (bf16[4,24,16,256]{3,2,1,0:T(8,128)(2,1)S(1)}, bf16[4,24,16,256]{3,2,1,0:T(8,128)(2,1)S(1)}, u32[]{:S(2)}, u32[]{:S(2)}) collective-permute-start(bf16[4,24,16,256]{3,2,1,0:T(8,128)(2,1)S(1)} %get-tuple-element.18), channel_id=1, source_target_pairs={{0,1},{1,0},{2,3},{3,2},{4,5},{5,4},{6,7},{7,6},{8,9},{9,8},{10,11... | collective-permute-start | bytes 2359304 | tf_op jit(solution)/shard_map/ppermute | solution.py:314
  15.5 8.6 %collective-permute-start.3 = (bf16[2,8,16,256]{3,2,1,0:T(8,128)(2,1)S(1)}, bf16[2,8,16,256]{3,2,1,0:T(8,128)(2,1)S(1)}, u32[]{:S(2)}, u32[]{:S(2)}) collective-permute-start(bf16[2,8,16,256]{3,2,1,0:T(8,128)(2,1)S(1)} %join.16), channel_id=1, source_target_pairs={{0,2},{1,3},{2,0},{3,1},{4,6},{5,7},{6,4},{7,5},{8,10},{9,11},{10,... | collective-permute-start | bytes 393224 | tf_op jit(solution)/shard_map/ppermute | solution.py:326
  18.5 13.0 %collective-permute-start.16 = (bf16[2,8,16,256]{3,2,1,0:T(8,128)(2,1)S(1)}, bf16[2,8,16,256]{3,2,1,0:T(8,128)(2,1)S(1)}, u32[]{:S(2)}, u32[]{:S(2)}) collective-permute-start(bf16[2,8,16,256]{3,2,1,0:T(8,128)(2,1)S(1)} %join.23), channel_id=1, source_target_pairs={{0,4},{1,5},{2,6},{3,7},{4,0},{5,1},{6,2},{7,3},{8,12},{9,13},{10,... | collective-permute-start | bytes 393224 | tf_op jit(solution)/shard_map/ppermute | solution.py:326
  21.2 10.3 %collective-permute-start.17 = (bf16[2,8,16,256]{3,2,1,0:T(8,128)(2,1)S(1)}, bf16[2,8,16,256]{3,2,1,0:T(8,128)(2,1)S(1)}, u32[]{:S(2)}, u32[]{:S(2)}) collective-permute-start(bf16[2,8,16,256]{3,2,1,0:T(8,128)(2,1)S(1)} %join.24), channel_id=1, source_target_pairs={{0,6},{1,7},{2,4},{3,5},{4,2},{5,3},{6,0},{7,1},{8,14},{9,15},{10,... | collective-permute-start | bytes 393224 | tf_op jit(solution)/shard_map/ppermute | solution.py:326
  21.3 12.3 %collective-permute-start.1 = (bf16[2,24,16,256]{3,2,1,0:T(8,128)(2,1)S(1)}, bf16[2,24,16,256]{3,2,1,0:T(8,128)(2,1)S(1)}, u32[]{:S(2)}, u32[]{:S(2)}) collective-permute-start(bf16[2,24,16,256]{3,2,1,0:T(8,128)(2,1)S(1)} %join.13.refs_0_), channel_id=1, source_target_pairs={{0,8},{8,24},{24,16},{16,0},{1,9},{9,25},{25,17},{17,1},{2,10},{10... | collective-permute-start | bytes 1179656 | tf_op jit(solution)/shard_map/ppermute | solution.py:270
  23.0 12.2 %collective-permute-start.2 = (bf16[2,24,16,256]{3,2,1,0:T(8,128)(2,1)S(1)}, bf16[2,24,16,256]{3,2,1,0:T(8,128)(2,1)S(1)}, u32[]{:S(2)}, u32[]{:S(2)}) collective-permute-start(bf16[2,24,16,256]{3,2,1,0:T(8,128)(2,1)S(1)} %join.13.refs_0_), channel_id=1, source_target_pairs={{8,0},{24,8},{16,24},{0,16},{9,1},{25,9},{17,25},{1,17},{10,2},{26... | collective-permute-start | bytes 1179656 | tf_op jit(solution)/shard_map/ppermute | solution.py:271
  31.5 11.2 %collective-permute-start.18 = (bf16[6,8,16,256]{3,2,1,0:T(8,128)(2,1)S(1)}, bf16[6,8,16,256]{3,2,1,0:T(8,128)(2,1)S(1)}, u32[]{:S(2)}, u32[]{:S(2)}) collective-permute-start(bf16[6,8,16,256]{3,2,1,0:T(8,128)(2,1)S(1)} %join.25.refs_1_), channel_id=1, source_target_pairs={{0,8},{8,24},{24,16},{16,0},{1,9},{9,25},{25,17},{17,1},{2,10},{10... | collective-permute-start | bytes 1179656 | tf_op jit(solution)/shard_map/ppermute | solution.py:270
  33.1 12.9 %collective-permute-start.19 = (bf16[6,8,16,256]{3,2,1,0:T(8,128)(2,1)S(1)}, bf16[6,8,16,256]{3,2,1,0:T(8,128)(2,1)S(1)}, u32[]{:S(2)}, u32[]{:S(2)}) collective-permute-start(bf16[6,8,16,256]{3,2,1,0:T(8,128)(2,1)S(1)} %join.25.refs_1_), channel_id=1, source_target_pairs={{8,0},{24,8},{16,24},{0,16},{9,1},{25,9},{17,25},{1,17},{10,2},{26... | collective-permute-start | bytes 1179656 | tf_op jit(solution)/shard_map/ppermute | solution.py:271
  33.6 17.4 %collective-permute-start.10 = (bf16[1,24,16,256]{3,2,1,0:T(8,128)(2,1)S(1)}, bf16[1,24,16,256]{3,2,1,0:T(8,128)(2,1)S(1)}, u32[]{:S(2)}, u32[]{:S(2)}) collective-permute-start(bf16[1,24,16,256]{3,2,1,0:T(8,128)(2,1)S(1)} %slice.32), channel_id=1, source_target_pairs={{0,8},{8,24},{24,16},{16,0},{1,9},{9,25},{25,17},{17,1},{2,10},{10... | collective-permute-start | bytes 589832 | tf_op jit(solution)/shard_map/ppermute | solution.py:284
  35.2 12.3 %collective-permute-start.13 = (bf16[2,8,16,256]{3,2,1,0:T(8,128)(2,1)S(1)}, bf16[2,8,16,256]{3,2,1,0:T(8,128)(2,1)S(1)}, u32[]{:S(2)}, u32[]{:S(2)}) collective-permute-start(bf16[2,8,16,256]{3,2,1,0:T(8,128)(2,1)S(1)} %join.21), channel_id=1, source_target_pairs={{0,6},{1,7},{2,4},{3,5},{4,2},{5,3},{6,0},{7,1},{8,14},{9,15},{10,... | collective-permute-start | bytes 393224 | tf_op jit(solution)/shard_map/ppermute | solution.py:326
  37.9 10.2 %collective-permute-start.12 = (bf16[2,8,16,256]{3,2,1,0:T(8,128)(2,1)S(1)}, bf16[2,8,16,256]{3,2,1,0:T(8,128)(2,1)S(1)}, u32[]{:S(2)}, u32[]{:S(2)}) collective-permute-start(bf16[2,8,16,256]{3,2,1,0:T(8,128)(2,1)S(1)} %join.20), channel_id=1, source_target_pairs={{0,4},{1,5},{2,6},{3,7},{4,0},{5,1},{6,2},{7,3},{8,12},{9,13},{10,... | collective-permute-start | bytes 393224 | tf_op jit(solution)/shard_map/ppermute | solution.py:326
  42.7 7.0 %collective-permute-start.4 = (bf16[2,8,16,256]{3,2,1,0:T(8,128)(2,1)S(1)}, bf16[2,8,16,256]{3,2,1,0:T(8,128)(2,1)S(1)}, u32[]{:S(2)}, u32[]{:S(2)}) collective-permute-start(bf16[2,8,16,256]{3,2,1,0:T(8,128)(2,1)S(1)} %join.15), channel_id=1, source_target_pairs={{0,2},{1,3},{2,0},{3,1},{4,6},{5,7},{6,4},{7,5},{8,10},{9,11},{10,... | collective-permute-start | bytes 393224 | tf_op jit(solution)/shard_map/ppermute | solution.py:326
  45.9 7.8 %collective-permute-start.11 = (bf16[1,24,16,256]{3,2,1,0:T(8,128)(2,1)S(1)}, bf16[1,24,16,256]{3,2,1,0:T(8,128)(2,1)S(1)}, u32[]{:S(2)}, u32[]{:S(2)}) collective-permute-start(bf16[1,24,16,256]{3,2,1,0:T(8,128)(2,1)S(1)} %slice.33), channel_id=1, source_target_pairs={{8,0},{24,8},{16,24},{0,16},{9,1},{25,9},{17,25},{1,17},{10,2},{26... | collective-permute-start | bytes 589832 | tf_op jit(solution)/shard_map/ppermute | solution.py:285
  47.5 7.9 %collective-permute-start.20 = (bf16[3,8,16,256]{3,2,1,0:T(8,128)(2,1)S(1)}, bf16[3,8,16,256]{3,2,1,0:T(8,128)(2,1)S(1)}, u32[]{:S(2)}, u32[]{:S(2)}) collective-permute-start(bf16[3,8,16,256]{3,2,1,0:T(8,128)(2,1)S(1)} %slice.34), channel_id=1, source_target_pairs={{0,8},{8,24},{24,16},{16,0},{1,9},{9,25},{25,17},{17,1},{2,10},{10... | collective-permute-start | bytes 589832 | tf_op jit(solution)/shard_map/ppermute | solution.py:284
  48.1 9.9 %collective-permute-start.21 = (bf16[3,8,16,256]{3,2,1,0:T(8,128)(2,1)S(1)}, bf16[3,8,16,256]{3,2,1,0:T(8,128)(2,1)S(1)}, u32[]{:S(2)}, u32[]{:S(2)}) collective-permute-start(bf16[3,8,16,256]{3,2,1,0:T(8,128)(2,1)S(1)} %slice.35), channel_id=1, source_target_pairs={{8,0},{24,8},{16,24},{0,16},{9,1},{25,9},{17,25},{1,17},{10,2},{26... | collective-permute-start | bytes 589832 | tf_op jit(solution)/shard_map/ppermute | solution.py:285
  49.7 16.5 %collective-permute-start.14 = (bf16[6,8,16,256]{3,2,1,0:T(8,128)(2,1)S(1)}, bf16[6,8,16,256]{3,2,1,0:T(8,128)(2,1)S(1)}, u32[]{:S(2)}, u32[]{:S(2)}) collective-permute-start(bf16[6,8,16,256]{3,2,1,0:T(8,128)(2,1)S(1)} %join.22.refs_1_), channel_id=1, source_target_pairs={{0,8},{8,24},{24,16},{16,0},{1,9},{9,25},{25,17},{17,1},{2,10},{10... | collective-permute-start | bytes 1179656 | tf_op jit(solution)/shard_map/ppermute | solution.py:270
  51.0 15.2 %collective-permute-start.15 = (bf16[6,8,16,256]{3,2,1,0:T(8,128)(2,1)S(1)}, bf16[6,8,16,256]{3,2,1,0:T(8,128)(2,1)S(1)}, u32[]{:S(2)}, u32[]{:S(2)}) collective-permute-start(bf16[6,8,16,256]{3,2,1,0:T(8,128)(2,1)S(1)} %join.22.refs_1_), channel_id=1, source_target_pairs={{8,0},{24,8},{16,24},{0,16},{9,1},{25,9},{17,25},{1,17},{10,2},{26... | collective-permute-start | bytes 1179656 | tf_op jit(solution)/shard_map/ppermute | solution.py:271
  53.8 14.6 %collective-permute-start.7 = (bf16[2,8,16,256]{3,2,1,0:T(8,128)(2,1)S(1)}, bf16[2,8,16,256]{3,2,1,0:T(8,128)(2,1)S(1)}, u32[]{:S(2)}, u32[]{:S(2)}) collective-permute-start(bf16[2,8,16,256]{3,2,1,0:T(8,128)(2,1)S(1)} %join.18), channel_id=1, source_target_pairs={{0,6},{1,7},{2,4},{3,5},{4,2},{5,3},{6,0},{7,1},{8,14},{9,15},{10,... | collective-permute-start | bytes 393224 | tf_op jit(solution)/shard_map/ppermute | solution.py:326
  55.4 13.0 %collective-permute-start.6 = (bf16[2,8,16,256]{3,2,1,0:T(8,128)(2,1)S(1)}, bf16[2,8,16,256]{3,2,1,0:T(8,128)(2,1)S(1)}, u32[]{:S(2)}, u32[]{:S(2)}) collective-permute-start(bf16[2,8,16,256]{3,2,1,0:T(8,128)(2,1)S(1)} %join.17), channel_id=1, source_target_pairs={{0,4},{1,5},{2,6},{3,7},{4,0},{5,1},{6,2},{7,3},{8,12},{9,13},{10,... | collective-permute-start | bytes 393224 | tf_op jit(solution)/shard_map/ppermute | solution.py:326
  58.0 10.4 %collective-permute-start.5 = (bf16[2,8,16,256]{3,2,1,0:T(8,128)(2,1)S(1)}, bf16[2,8,16,256]{3,2,1,0:T(8,128)(2,1)S(1)}, u32[]{:S(2)}, u32[]{:S(2)}) collective-permute-start(bf16[2,8,16,256]{3,2,1,0:T(8,128)(2,1)S(1)} %join.14), channel_id=1, source_target_pairs={{0,2},{1,3},{2,0},{3,1},{4,6},{5,7},{6,4},{7,5},{8,10},{9,11},{10,... | collective-permute-start | bytes 393224 | tf_op jit(solution)/shard_map/ppermute | solution.py:326
  66.2 6.8 %collective-permute-start.22 = (bf16[3,8,16,256]{3,2,1,0:T(8,128)(2,1)S(1)}, bf16[3,8,16,256]{3,2,1,0:T(8,128)(2,1)S(1)}, u32[]{:S(2)}, u32[]{:S(2)}) collective-permute-start(bf16[3,8,16,256]{3,2,1,0:T(8,128)(2,1)S(1)} %slice.28), channel_id=1, source_target_pairs={{0,8},{8,24},{24,16},{16,0},{1,9},{9,25},{25,17},{17,1},{2,10},{10... | collective-permute-start | bytes 589832 | tf_op jit(solution)/shard_map/ppermute | solution.py:284
  67.7 6.7 %collective-permute-start.23 = (bf16[3,8,16,256]{3,2,1,0:T(8,128)(2,1)S(1)}, bf16[3,8,16,256]{3,2,1,0:T(8,128)(2,1)S(1)}, u32[]{:S(2)}, u32[]{:S(2)}) collective-permute-start(bf16[3,8,16,256]{3,2,1,0:T(8,128)(2,1)S(1)} %slice.29), channel_id=1, source_target_pairs={{8,0},{24,8},{16,24},{0,16},{9,1},{25,9},{17,25},{1,17},{10,2},{26... | collective-permute-start | bytes 589832 | tf_op jit(solution)/shard_map/ppermute | solution.py:285
  68.4 13.8 %collective-permute-start.8 = (bf16[6,8,16,256]{3,2,1,0:T(8,128)(2,1)S(1)}, bf16[6,8,16,256]{3,2,1,0:T(8,128)(2,1)S(1)}, u32[]{:S(2)}, u32[]{:S(2)}) collective-permute-start(bf16[6,8,16,256]{3,2,1,0:T(8,128)(2,1)S(1)} %join.19.refs_1_), channel_id=1, source_target_pairs={{0,8},{8,24},{24,16},{16,0},{1,9},{9,25},{25,17},{17,1},{2,10},{10... | collective-permute-start | bytes 1179656 | tf_op jit(solution)/shard_map/ppermute | solution.py:270
  69.8 12.4 %collective-permute-start.9 = (bf16[6,8,16,256]{3,2,1,0:T(8,128)(2,1)S(1)}, bf16[6,8,16,256]{3,2,1,0:T(8,128)(2,1)S(1)}, u32[]{:S(2)}, u32[]{:S(2)}) collective-permute-start(bf16[6,8,16,256]{3,2,1,0:T(8,128)(2,1)S(1)} %join.19.refs_1_), channel_id=1, source_target_pairs={{8,0},{24,8},{16,24},{0,16},{9,1},{25,9},{17,25},{1,17},{10,2},{26... | collective-permute-start | bytes 1179656 | tf_op jit(solution)/shard_map/ppermute | solution.py:271
  82.3 5.7 %collective-permute-start.24 = (bf16[3,8,16,256]{3,2,1,0:T(8,128)(2,1)S(1)}, bf16[3,8,16,256]{3,2,1,0:T(8,128)(2,1)S(1)}, u32[]{:S(2)}, u32[]{:S(2)}) collective-permute-start(bf16[3,8,16,256]{3,2,1,0:T(8,128)(2,1)S(1)} %slice.30), channel_id=1, source_target_pairs={{0,8},{8,24},{24,16},{16,0},{1,9},{9,25},{25,17},{17,1},{2,10},{10... | collective-permute-start | bytes 589832 | tf_op jit(solution)/shard_map/ppermute | solution.py:284
  83.0 5.7 %collective-permute-start.25 = (bf16[3,8,16,256]{3,2,1,0:T(8,128)(2,1)S(1)}, bf16[3,8,16,256]{3,2,1,0:T(8,128)(2,1)S(1)}, u32[]{:S(2)}, u32[]{:S(2)}) collective-permute-start(bf16[3,8,16,256]{3,2,1,0:T(8,128)(2,1)S(1)} %slice.31), channel_id=1, source_target_pairs={{8,0},{24,8},{16,24},{0,16},{9,1},{25,9},{17,25},{1,17},{10,2},{26... | collective-permute-start | bytes 589832 | tf_op jit(solution)/shard_map/ppermute | solution.py:285
where the time goes:
time: 96.8 us; the launch traced here: 96.6 us
  Pallas kernels  37.2 us (38%)
  starting transfers between devices  34.2 us (35%)
  waiting for transfers between devices  22.7 us (23%)
  local copies, waits for them, and re-layouts  2.35 us (2%)
    pallas_call x3, Pallas kernels, stack(): pl.pallas_call(functools.partial(stack_kernel, windows, 1.0 / math.sqrt(s...  23.7 us
    ppermute x9, starting transfers between devices, local(): lax.ppermute(sent, 'win', [(i, i ^ 2 * k) for i in range(dests)])  15.8 us
    pallas_call x1, Pallas kernels, spectra(): pl.pallas_call(spectra_kernel, in_specs=[pl.BlockSpec(memory_space=pltpu....  10.8 us
    ppermute x9, waiting for transfers between devices, local(): lax.ppermute(sent, 'win', [(i, i ^ 2 * k) for i in range(dests)])  8.12 us
    ppermute x4, starting transfers between devices, ring_start(): left = lax.ppermute(left, 'chan', ahead)  5.99 us
    ppermute x4, starting transfers between devices, ring_finish(): second = lax.ppermute(right[cut_at:], 'chan', [(b, a) for a, b in ahead])  5.34 us
    ppermute x4, waiting for transfers between devices, ring_finish(): second = lax.ppermute(right[cut_at:], 'chan', [(b, a) for a, b in ahead])  4.57 us
    ppermute x4, waiting for transfers between devices, ring_finish(): first = lax.ppermute(left[:cut_at], 'chan', ahead)  4.45 us
  transfers between devices with their start and end apart: 26, of which 10 were waited for; matrix products, arithmetic and copies ran while one was open for 0% of the time, Pallas kernels for 19%

commit v1 on v0

--- a/solution.py
+++ b/solution.py
@@ -31,13 +31,11 @@
 
 def interleave(windows, bins):
     pair = 16 // (2 * windows)
-    out = np.zeros((2 * windows * bins, 2 * windows * bins), np.float32)
-    for f in range(bins):
-        for p in range(2):
-            for w in range(windows):
-                row = ((f // pair * 2 + p) * pair + f % pair) * windows + w
-                out[row, (w * 2 + p) * bins + f] = 1.0
-    return out.astype(ml_dtypes.bfloat16)
+    rows = 2 * windows * bins
+    row = lax.broadcasted_iota(jnp.int32, (rows, rows), 0)
+    col = lax.broadcasted_iota(jnp.int32, (rows, rows), 1)
+    w, b, p, g = row % windows, row // windows % pair, row // 8 % 2, row // 16
+    return jnp.where(col == (w * 2 + p) * bins + g * pair + b, 1.0, 0.0).astype(jnp.bfloat16)
 
 
 def cut(raw_ref, slot, shift_at, window_ref):
@@ -61,22 +59,23 @@
         window_ref[step * tile : (step + 1) * tile, :] = moved.reshape(tile, width).astype(jnp.bfloat16)
 
 
-def spectra_kernel(offsets_ref, table_hbm, mix_hbm, raw_hbm, quality_hbm, keep_ref, give_ref, *scratch):
-    table_ref, mix_ref, quality_ref, raw_ref, white, mixed, sems = scratch[:7]
-    cuts = scratch[7:]
+def spectra_kernel(offsets_ref, table_hbm, raw_hbm, quality_hbm, keep_ref, give_ref, *scratch):
+    table_ref, quality_ref, raw_ref, white, mixed, sems = scratch[:6]
+    cuts = scratch[6:]
     windows, _, width = raw_ref.shape
     loads = [pltpu.make_async_copy(raw_hbm.at[w], raw_ref.at[w], sems.at[w]) for w in range(windows)]
     table_load = pltpu.make_async_copy(table_hbm, table_ref, sems.at[windows])
-    mix_load = pltpu.make_async_copy(mix_hbm, mix_ref, sems.at[windows + 1])
-    quality_load = pltpu.make_async_copy(quality_hbm, quality_ref, sems.at[windows + 2])
-    for load in (loads[0], table_load, *loads[1:], quality_load, mix_load):
+    quality_load = pltpu.make_async_copy(quality_hbm, quality_ref, sems.at[windows + 1])
+    for load in (loads[0], quality_load, table_load, *loads[1:]):
         load.start()
     loads[0].wait()
     cut(raw_ref, 0, offsets_ref[0], cuts[0])
-    for load in (table_load, *loads[1:], quality_load, mix_load):
-        load.wait()
+    mix = interleave(windows, 256 // (2 * windows))
+    quality_load.wait()
+    table_load.wait()
     for w in range(windows):
         if w + 1 < windows:
+            loads[w + 1].wait()
             cut(raw_ref, w + 1, offsets_ref[w + 1], cuts[w + 1])
         transform = jnp.dot(table_ref[...], cuts[w][...], preferred_element_type=jnp.float32)
         band_power = jnp.sum(transform * transform, axis=0, keepdims=True) / F
@@ -84,13 +83,13 @@
         white[w] = (transform * (lax.rsqrt(band_power + epsilon) * usable)).astype(jnp.bfloat16)
 
     pair = 16 // (2 * windows)
-    bins = mix_ref.shape[0] // (2 * windows)
+    bins = mix.shape[0] // (2 * windows)
     groups = bins // pair
     for block in range(F // bins):
         parts = [
             white[v, p * F + block * bins : p * F + (block + 1) * bins, :] for v in range(windows) for p in range(2)
         ]
-        product = jnp.dot(mix_ref[...], jnp.concatenate(parts, 0), preferred_element_type=jnp.float32)
+        product = jnp.dot(mix, jnp.concatenate(parts, 0), preferred_element_type=jnp.float32)
         mixed[block * groups : (block + 1) * groups] = product.astype(jnp.bfloat16).reshape(groups, 16, width)
     me = lax.axis_index("win")
     chip, core = me // 2, me % 2
@@ -105,22 +104,21 @@
     return [pl.BlockSpec(memory_space=pltpu.VMEM)] * count
 
 
-def spectra(raw, offsets, quality, table, mix, dests):
+def spectra(raw, offsets, quality, table, dests):
     windows, _, width = raw.shape
     groups = F * 2 * windows // 16
     blocks = (dests // 2, groups // dests, 16, width)
     return pl.pallas_call(
         spectra_kernel,
-        in_specs=[pl.BlockSpec(memory_space=pltpu.SMEM)] + [pl.BlockSpec(memory_space=pl.ANY)] * 4,
+        in_specs=[pl.BlockSpec(memory_space=pltpu.SMEM)] + [pl.BlockSpec(memory_space=pl.ANY)] * 3,
         out_specs=in_vmem(2),
         scratch_shapes=[
             pltpu.VMEM(table.shape, table.dtype),
-            pltpu.VMEM(mix.shape, mix.dtype),
             pltpu.VMEM(quality.shape, quality.dtype),
             pltpu.VMEM(raw.shape, raw.dtype),
             pltpu.VMEM((windows, 2 * F, width), jnp.bfloat16),
             pltpu.VMEM((groups, 16, width), jnp.bfloat16),
-            pltpu.SemaphoreType.DMA((windows + 3,)),
+            pltpu.SemaphoreType.DMA((windows + 2,)),
             *[pltpu.VMEM((L, width), jnp.bfloat16)] * windows,
         ],
         out_shape=[jax.ShapeDtypeStruct(blocks, jnp.bfloat16)] * 2,
@@ -129,7 +127,7 @@
             flops=2 * windows * 2 * F * L * width, bytes_accessed=2 * windows * raw.shape[1] * width + 4 * F * L, transcendentals=0
         ),
         name="spectra",
-    )(offsets, table, mix, raw, quality)
+    )(offsets, table, raw, quality)
 
 
 def join_kernel(moves, *refs):
@@ -164,29 +162,33 @@
     return ref[sources[0] : sources[1], group - at].reshape(-1, ref.shape[-1])
 
 
-def turn_kernel(first_group, views, *refs):
+def turn_kernel(windows, first_group, views, *refs):
     out_ref = refs[-1]
-    _, _, width, depth = out_ref.shape
+    _, pair, _, width, depth = out_ref.shape
+    bin_of = lax.broadcasted_iota(jnp.int32, (width, depth), 1) % 8 // windows
 
     def body(g, carry):
         x = jnp.concatenate([view(refs[i], first_group + g, *where) for i, where in enumerate(views)], 0)
         by_part = x.astype(jnp.float32).reshape(depth // 16, 16, width)
         turned = jnp.concatenate([by_part[:, 8:], -by_part[:, :8]], 1)
-        out_ref[g, 0] = by_part.reshape(depth, width).T.astype(jnp.bfloat16)
-        out_ref[g, 1] = turned.reshape(depth, width).T.astype(jnp.bfloat16)
+        for part, rows in enumerate((by_part, turned)):
+            left = rows.reshape(depth, width).T
+            for b in range(pair):
+                out_ref[g, b, part] = jnp.where(bin_of == b, left, 0.0).astype(jnp.bfloat16)
         return carry
 
     lax.fori_loop(0, out_ref.shape[0], body, 0)
 
 
-def turn(items, first_group, groups):
+def turn(items, first_group, groups, windows):
     rows, width = items[0][0].shape[2:]
     depth = sum(sources[1] - sources[0] for _, _, sources in items) * rows
+    pair = 16 // (2 * windows)
     return pl.pallas_call(
-        functools.partial(turn_kernel, first_group, [item[1:] for item in items]),
+        functools.partial(turn_kernel, windows, first_group, [item[1:] for item in items]),
         in_specs=in_vmem(len(items)),
         out_specs=in_vmem(1)[0],
-        out_shape=jax.ShapeDtypeStruct((groups, 2, width, depth), jnp.bfloat16),
+        out_shape=jax.ShapeDtypeStruct((groups, pair, 2, width, depth), jnp.bfloat16),
         compiler_params=pltpu.CompilerParams(vmem_limit_bytes=12 * MIB),
         cost_estimate=pl.CostEstimate(flops=0, bytes_accessed=8 * groups * width * depth, transcendentals=0),
         name="turn",
@@ -197,32 +199,28 @@
     return jnp.where(i < members // 2, i, members - 1 - i + members // 2)
 
 
-def stack_kernel(windows, scale, first_group, layout, left_ref, *refs):
+def stack_kernel(scale, left_first, first_group, layout, left_ref, *refs):
     out_ref = refs[-1]
-    pair = 16 // (2 * windows)
-    width, depth = left_ref.shape[2:]
+    pair, _, width, _ = left_ref.shape[1:]
     step_groups = out_ref.shape[0] // pair
     members = len(layout)
     where = closed_walk(lax.axis_index("chan"), members)
-    bin_of = lax.broadcasted_iota(jnp.int32, (width, depth), 1) % 8 // windows
-    masks = [jnp.where(bin_of == b, 1.0, 0.0).astype(jnp.bfloat16) for b in range(pair)]
     for s in range(step_groups):
         g = pl.program_id(0) * step_groups + s
-        sides = [left_ref[g, part] for part in range(2)]
         for step, items in layout:
             right = jnp.concatenate([view(refs[i], first_group + g, *item) for i, item in items], 0)
             column = closed_walk(lax.rem(where + (step + members), members), members)
             columns = pl.ds(pl.multiple_of(column * width, width), width)
             for b in range(pair):
                 for part in range(2):
-                    product = jnp.dot(sides[part] * masks[b], right, preferred_element_type=jnp.float32)
+                    left = left_ref[first_group - left_first + g, b, part]
+                    product = jnp.dot(left, right, preferred_element_type=jnp.float32)
                     out_ref[s * pair + b, part, :, columns] = (product * scale).astype(jnp.bfloat16)
 
 
-def stack(left, steps, into, first_group, bins, windows, sources):
+def stack(left, left_first, steps, into, first_group, groups, bins, sources):
     members = len(steps)
-    groups, _, width, depth = left.shape
-    pair = 16 // (2 * windows)
+    _, pair, _, width, depth = left.shape
     step_groups = max(n for n in range(1, STEP_GROUPS + 1) if groups % n == 0 and first_group % n == 0)
     operands, layout = [left], []
     for step, items in steps:
@@ -236,7 +234,7 @@
         in_specs.append(pl.BlockSpec(memory_space=pl.ANY))
     block = (step_groups * pair, 2, width, members * width)
     return pl.pallas_call(
-        functools.partial(stack_kernel, windows, 1.0 / math.sqrt(sources), first_group, layout),
+        functools.partial(stack_kernel, 1.0 / math.sqrt(sources), left_first, first_group, layout),
         grid=(groups // step_groups,),
         in_specs=in_specs,
         out_specs=pl.BlockSpec(block, lambda g: (first_group // step_groups + g, 0, 0, 0)),
@@ -308,9 +306,8 @@
     starts = chunk_starts(share)
     chunks = list(zip(starts[:-1], starts[1:]))
     table = jnp.asarray(dft_table())
-    mix = jnp.asarray(interleave(windows, 256 // (2 * windows)))
-
-    keep, give = spectra(raw, offsets, quality, table, mix, dests)
+
+    keep, give = spectra(raw, offsets, quality, table, dests)
     other = lax.ppermute(give, "win", [(i, i ^ 1) for i in range(dests)])
     own = join([(keep, 0, 0, 1), (other, 0, 0, 1)], share)
     own_start = ring_start(own, members)
@@ -335,8 +332,8 @@
         for (step, own_arrays), (_, arrays) in zip(own_blocks, blocks):
             views = [(x, 0, (0, x.shape[0])) for x in own_arrays] + [(x, start, (0, x.shape[0])) for x in arrays]
             steps.append((step, views))
-        left = turn(steps[0][1], start, stop - start)
-        out = stack(left, steps, out, start, bins, windows, dests * windows)
+        left = turn(steps[0][1], start, stop - start, windows)
+        out = stack(left, start, steps, out, start, stop - start, bins, dests * windows)
     return out
 
 

time: 96.8 us -> 99.4 us (1.027)
  Pallas kernels: 37.2 us -> 40.8 us
    pallas_call x1, Pallas kernels: 10.8 us -> 14.3 us  [spectra(): pl.pallas_call(spectra_kernel, in_specs=[pl.BlockSpec(memory_space=pltpu....]
    unnamed x6 -> x4, local copies, waits for them, and re-layouts: 2.24 us -> 1.34 us
where the time goes in v1:
time: 99.4 us; the launch traced here: 99.2 us
  Pallas kernels  40.8 us (41%)
  starting transfers between devices  34.1 us (34%)
  waiting for transfers between devices  22.6 us (23%)
  local copies, waits for them, and re-layouts  1.45 us (1%)
    pallas_call x3, Pallas kernels, stack(): pl.pallas_call(functools.partial(stack_kernel, 1.0 / math.sqrt(sources),...  23.7 us
    ppermute x9, starting transfers between devices, local(): lax.ppermute(sent, 'win', [(i, i ^ 2 * k) for i in range(dests)])  15.8 us
    pallas_call x1, Pallas kernels, spectra(): pl.pallas_call(spectra_kernel, in_specs=[pl.BlockSpec(memory_space=pltpu....  14.3 us
    ppermute x9, waiting for transfers between devices, local(): lax.ppermute(sent, 'win', [(i, i ^ 2 * k) for i in range(dests)])  8.11 us
    ppermute x4, starting transfers between devices, ring_start(): left = lax.ppermute(left, 'chan', ahead)  5.98 us
    ppermute x4, starting transfers between devices, ring_finish(): second = lax.ppermute(right[cut_at:], 'chan', [(b, a) for a, b in ahead])  5.36 us
    ppermute x4, waiting for transfers between devices, ring_finish(): second = lax.ppermute(right[cut_at:], 'chan', [(b, a) for a, b in ahead])  4.56 us
    ppermute x4, waiting for transfers between devices, ring_finish(): first = lax.ppermute(left[:cut_at], 'chan', ahead)  4.36 us
  transfers between devices with their start and end apart: 26, of which 10 were waited for; matrix products, arithmetic and copies ran while one was open for 0% of the time, Pallas kernels for 19%

profile of v1, /device:TPU:0, one launch (start us, length us, event | category | flops | bytes accessed | tf_op | source)
XLA Modules:
  0.0 99.2 jit_solution(2119539145981083613)
XLA Ops:
  0.0 0.0 copy-start
  0.0 0.7 copy-done
  0.7 0.0 copy-start.1
  0.7 0.7 copy-done.1
  1.3 14.3 %spectra.1 = (bf16[4,24,16,256]{3,2,1,0:T(8,128)(2,1)S(1)}, bf16[4,24,16,256]{3,2,1,0:T(8,128)(2,1)S(1)}) custom-call(s32[4]{0:T(128)S(1)} %copy-done.1, bf16[768,3072]{1,0:T(8,128)(2,1)} %constant.2.clone.table_hbm, bf16[4,3200,256]{2,1,0:T(8,128)(2,1)} %raw_hbm.1, s32[4,256]{1,0:T(4,128)S(1)} %copy-done), custom_call_target="tpu_custom_call" | custom-call | flops 4831838208 | bytes 11272192 | tf_op jit(solution)/shard_map/spectra/pallas_call | solution.py:111
  15.7 0.5 collective-permute-start
  16.2 1.9 %collective-permute-done.refs_1_ = bf16[4,24,16,256]{3,2,1,0:T(8,128)(2,1)S(1)} collective-permute-done((bf16[4,24,16,256]{3,2,1,0:T(8,128)(2,1)S(1)}, bf16[4,24,16,256]{3,2,1,0:T(8,128)(2,1)S(1)}, u32[]{:S(2)}, u32[]{:S(2)}) %collective-permute-start) | collective-permute-done | bytes 786464 | tf_op jit(solution)/shard_map/ppermute | solution.py:311
  18.1 3.0 %collective-permute-start.3 = (bf16[2,8,16,256]{3,2,1,0:T(8,128)(2,1)S(1)}, bf16[2,8,16,256]{3,2,1,0:T(8,128)(2,1)S(1)}, u32[]{:S(2)}, u32[]{:S(2)}) collective-permute-start(bf16[2,8,16,256]{3,2,1,0:T(8,128)(2,1)S(1)} %join.16), channel_id=1, source_target_pairs={{0,2},{1,3},{2,0},{3,1},{4,6},{5,7},{6,4},{7,5},{8,10},{9,11},{10,... | collective-permute-start | bytes 393224 | tf_op jit(solution)/shard_map/ppermute | solution.py:323
  21.1 2.7 %collective-permute-start.16 = (bf16[2,8,16,256]{3,2,1,0:T(8,128)(2,1)S(1)}, bf16[2,8,16,256]{3,2,1,0:T(8,128)(2,1)S(1)}, u32[]{:S(2)}, u32[]{:S(2)}) collective-permute-start(bf16[2,8,16,256]{3,2,1,0:T(8,128)(2,1)S(1)} %join.23), channel_id=1, source_target_pairs={{0,4},{1,5},{2,6},{3,7},{4,0},{5,1},{6,2},{7,3},{8,12},{9,13},{10,... | collective-permute-start | bytes 393224 | tf_op jit(solution)/shard_map/ppermute | solution.py:323
  23.8 0.1 collective-permute-start.17
  23.9 1.7 %collective-permute-start.1 = (bf16[2,24,16,256]{3,2,1,0:T(8,128)(2,1)S(1)}, bf16[2,24,16,256]{3,2,1,0:T(8,128)(2,1)S(1)}, u32[]{:S(2)}, u32[]{:S(2)}) collective-permute-start(bf16[2,24,16,256]{3,2,1,0:T(8,128)(2,1)S(1)} %join.13.refs_0_), channel_id=1, source_target_pairs={{0,8},{8,24},{24,16},{16,0},{1,9},{9,25},{25,17},{17,1},{2,10},{10... | collective-permute-start | bytes 1179656 | tf_op jit(solution)/shard_map/ppermute | solution.py:268
  25.7 0.3 collective-permute-start.2
  26.0 0.7 collective-permute-done.3.refs_0_
  26.8 7.3 %collective-permute-done.16.refs_1_ = bf16[2,8,16,256]{3,2,1,0:T(8,128)(2,1)S(1)} collective-permute-done((bf16[2,8,16,256]{3,2,1,0:T(8,128)(2,1)S(1)}, bf16[2,8,16,256]{3,2,1,0:T(8,128)(2,1)S(1)}, u32[]{:S(2)}, u32[]{:S(2)}) %collective-permute-start.16) | collective-permute-done | bytes 131104 | tf_op jit(solution)/shard_map/ppermute | solution.py:323
  34.1 0.0 collective-permute-done.17.refs_2_
  34.1 1.5 %collective-permute-start.18 = (bf16[6,8,16,256]{3,2,1,0:T(8,128)(2,1)S(1)}, bf16[6,8,16,256]{3,2,1,0:T(8,128)(2,1)S(1)}, u32[]{:S(2)}, u32[]{:S(2)}) collective-permute-start(bf16[6,8,16,256]{3,2,1,0:T(8,128)(2,1)S(1)} %join.25.refs_1_), channel_id=1, source_target_pairs={{0,8},{8,24},{24,16},{16,0},{1,9},{9,25},{25,17},{17,1},{2,10},{10... | collective-permute-start | bytes 1179656 | tf_op jit(solution)/shard_map/ppermute | solution.py:268
  35.7 0.5 collective-permute-start.19
  36.2 0.0 collective-permute-done.1.refs_2_
  36.2 1.5 %collective-permute-start.10 = (bf16[1,24,16,256]{3,2,1,0:T(8,128)(2,1)S(1)}, bf16[1,24,16,256]{3,2,1,0:T(8,128)(2,1)S(1)}, u32[]{:S(2)}, u32[]{:S(2)}) collective-permute-start(bf16[1,24,16,256]{3,2,1,0:T(8,128)(2,1)S(1)} %slice.32), channel_id=1, source_target_pairs={{0,8},{8,24},{24,16},{16,0},{1,9},{9,25},{25,17},{17,1},{2,10},{10... | collective-permute-start | bytes 589832 | tf_op jit(solution)/shard_map/ppermute | solution.py:282
  37.8 0.0 collective-permute-done.2.refs_4_
  37.8 2.7 %collective-permute-start.13 = (bf16[2,8,16,256]{3,2,1,0:T(8,128)(2,1)S(1)}, bf16[2,8,16,256]{3,2,1,0:T(8,128)(2,1)S(1)}, u32[]{:S(2)}, u32[]{:S(2)}) collective-permute-start(bf16[2,8,16,256]{3,2,1,0:T(8,128)(2,1)S(1)} %join.21), channel_id=1, source_target_pairs={{0,6},{1,7},{2,4},{3,5},{4,2},{5,3},{6,0},{7,1},{8,14},{9,15},{10,... | collective-permute-start | bytes 393224 | tf_op jit(solution)/shard_map/ppermute | solution.py:323
  40.6 1.1 %collective-permute-start.12 = (bf16[2,8,16,256]{3,2,1,0:T(8,128)(2,1)S(1)}, bf16[2,8,16,256]{3,2,1,0:T(8,128)(2,1)S(1)}, u32[]{:S(2)}, u32[]{:S(2)}) collective-permute-start(bf16[2,8,16,256]{3,2,1,0:T(8,128)(2,1)S(1)} %join.20), channel_id=1, source_target_pairs={{0,4},{1,5},{2,6},{3,7},{4,0},{5,1},{6,2},{7,3},{8,12},{9,13},{10,... | collective-permute-start | bytes 393224 | tf_op jit(solution)/shard_map/ppermute | solution.py:323
  41.6 3.7 %collective-permute-done.18.refs_3_ = bf16[6,8,16,256]{3,2,1,0:T(8,128)(2,1)S(1)} collective-permute-done((bf16[6,8,16,256]{3,2,1,0:T(8,128)(2,1)S(1)}, bf16[6,8,16,256]{3,2,1,0:T(8,128)(2,1)S(1)}, u32[]{:S(2)}, u32[]{:S(2)}) %collective-permute-start.18) | collective-permute-done | bytes 393248 | tf_op jit(solution)/shard_map/ppermute | solution.py:268
  45.3 3.2 %collective-permute-start.4 = (bf16[2,8,16,256]{3,2,1,0:T(8,128)(2,1)S(1)}, bf16[2,8,16,256]{3,2,1,0:T(8,128)(2,1)S(1)}, u32[]{:S(2)}, u32[]{:S(2)}) collective-permute-start(bf16[2,8,16,256]{3,2,1,0:T(8,128)(2,1)S(1)} %join.15), channel_id=1, source_target_pairs={{0,2},{1,3},{2,0},{3,1},{4,6},{5,7},{6,4},{7,5},{8,10},{9,11},{10,... | collective-permute-start | bytes 393224 | tf_op jit(solution)/shard_map/ppermute | solution.py:323
  48.5 0.0 collective-permute-done.19.refs_5_
  48.6 1.6 %collective-permute-start.11 = (bf16[1,24,16,256]{3,2,1,0:T(8,128)(2,1)S(1)}, bf16[1,24,16,256]{3,2,1,0:T(8,128)(2,1)S(1)}, u32[]{:S(2)}, u32[]{:S(2)}) collective-permute-start(bf16[1,24,16,256]{3,2,1,0:T(8,128)(2,1)S(1)} %slice.33), channel_id=1, source_target_pairs={{8,0},{24,8},{16,24},{0,16},{9,1},{25,9},{17,25},{1,17},{10,2},{26... | collective-permute-start | bytes 589832 | tf_op jit(solution)/shard_map/ppermute | solution.py:283
  50.1 0.0 collective-permute-done.13.refs_2_
  50.2 0.6 collective-permute-start.20
  50.7 0.0 collective-permute-done.12.refs_1_
  50.7 1.6 %collective-permute-start.21 = (bf16[3,8,16,256]{3,2,1,0:T(8,128)(2,1)S(1)}, bf16[3,8,16,256]{3,2,1,0:T(8,128)(2,1)S(1)}, u32[]{:S(2)}, u32[]{:S(2)}) collective-permute-start(bf16[3,8,16,256]{3,2,1,0:T(8,128)(2,1)S(1)} %slice.35), channel_id=1, source_target_pairs={{8,0},{24,8},{16,24},{0,16},{9,1},{25,9},{17,25},{1,17},{10,2},{26... | collective-permute-start | bytes 589832 | tf_op jit(solution)/shard_map/ppermute | solution.py:283
  52.3 0.0 collective-permute-done.4.refs_0_
  52.3 1.3 %collective-permute-start.14 = (bf16[6,8,16,256]{3,2,1,0:T(8,128)(2,1)S(1)}, bf16[6,8,16,256]{3,2,1,0:T(8,128)(2,1)S(1)}, u32[]{:S(2)}, u32[]{:S(2)}) collective-permute-start(bf16[6,8,16,256]{3,2,1,0:T(8,128)(2,1)S(1)} %join.22.refs_1_), channel_id=1, source_target_pairs={{0,8},{8,24},{24,16},{16,0},{1,9},{9,25},{25,17},{17,1},{2,10},{10... | collective-permute-start | bytes 1179656 | tf_op jit(solution)/shard_map/ppermute | solution.py:268
  53.7 0.0 collective-permute-done.10.refs_6_
  53.7 0.7 collective-permute-start.15
  54.5 0.9 turn.5.left_ref
  55.4 1.0 %collective-permute-done.11.refs_7_ = bf16[1,24,16,256]{3,2,1,0:T(8,128)(2,1)S(1)} collective-permute-done((bf16[1,24,16,256]{3,2,1,0:T(8,128)(2,1)S(1)}, bf16[1,24,16,256]{3,2,1,0:T(8,128)(2,1)S(1)}, u32[]{:S(2)}, u32[]{:S(2)}) %collective-permute-start.11) | collective-permute-done | bytes 196640 | tf_op jit(solution)/shard_map/ppermute | solution.py:283
  56.4 1.7 %collective-permute-start.7 = (bf16[2,8,16,256]{3,2,1,0:T(8,128)(2,1)S(1)}, bf16[2,8,16,256]{3,2,1,0:T(8,128)(2,1)S(1)}, u32[]{:S(2)}, u32[]{:S(2)}) collective-permute-start(bf16[2,8,16,256]{3,2,1,0:T(8,128)(2,1)S(1)} %join.18), channel_id=1, source_target_pairs={{0,6},{1,7},{2,4},{3,5},{4,2},{5,3},{6,0},{7,1},{8,14},{9,15},{10,... | collective-permute-start | bytes 393224 | tf_op jit(solution)/shard_map/ppermute | solution.py:323
  58.1 0.0 collective-permute-done.20.refs_8_
  58.1 1.0 %collective-permute-start.6 = (bf16[2,8,16,256]{3,2,1,0:T(8,128)(2,1)S(1)}, bf16[2,8,16,256]{3,2,1,0:T(8,128)(2,1)S(1)}, u32[]{:S(2)}, u32[]{:S(2)}) collective-permute-start(bf16[2,8,16,256]{3,2,1,0:T(8,128)(2,1)S(1)} %join.17), channel_id=1, source_target_pairs={{0,4},{1,5},{2,6},{3,7},{4,0},{5,1},{6,2},{7,3},{8,12},{9,13},{10,... | collective-permute-start | bytes 393224 | tf_op jit(solution)/shard_map/ppermute | solution.py:323
  59.1 1.5 %collective-permute-done.21.refs_9_ = bf16[3,8,16,256]{3,2,1,0:T(8,128)(2,1)S(1)} collective-permute-done((bf16[3,8,16,256]{3,2,1,0:T(8,128)(2,1)S(1)}, bf16[3,8,16,256]{3,2,1,0:T(8,128)(2,1)S(1)}, u32[]{:S(2)}, u32[]{:S(2)}) %collective-permute-start.21) | collective-permute-done | bytes 196640 | tf_op jit(solution)/shard_map/ppermute | solution.py:283
  60.6 0.4 collective-permute-start.5
  61.0 7.9 %stack.3.refs_10_ = bf16[48,2,256,1024]{3,2,1,0:T(8,128)(2,1)} custom-call(bf16[8,2,2,256,128]{4,3,2,1,0:T(8,128)(2,1)S(1)} %turn.5.left_ref, bf16[2,24,16,256]{3,2,1,0:T(8,128)(2,1)S(1)} %join.13.refs_0_, bf16[6,8,16,256]{3,2,1,0:T(8,128)(2,1)S(1)} %join.25.refs_1_, bf16[2,24,16,256]{3,2,1,0:T(8,128)(2,1)S(1)} %collective-permute-done.1.refs_2_, ...), custom_call_target="tpu_custom_call" | custom-call | flops 2147483648 | bytes 16777216 | tf_op jit(solution)/shard_map/stack/pallas_call | solution.py:236
  68.9 0.0 collective-permute-done.14.refs_3_
  68.9 0.0 collective-permute-done.15.refs_5_
  68.9 1.4 %collective-permute-start.22 = (bf16[3,8,16,256]{3,2,1,0:T(8,128)(2,1)S(1)}, bf16[3,8,16,256]{3,2,1,0:T(8,128)(2,1)S(1)}, u32[]{:S(2)}, u32[]{:S(2)}) collective-permute-start(bf16[3,8,16,256]{3,2,1,0:T(8,128)(2,1)S(1)} %slice.28), channel_id=1, source_target_pairs={{0,8},{8,24},{24,16},{16,0},{1,9},{9,25},{25,17},{17,1},{2,10},{10... | collective-permute-start | bytes 589832 | tf_op jit(solution)/shard_map/ppermute | solution.py:282
  70.2 0.8 collective-permute-start.23
  71.0 0.0 collective-permute-done.7.refs_2_
  71.0 0.0 collective-permute-done.6.refs_1_
  71.0 0.0 collective-permute-done.5.refs_0_
  71.1 1.4 %collective-permute-start.8 = (bf16[6,8,16,256]{3,2,1,0:T(8,128)(2,1)S(1)}, bf16[6,8,16,256]{3,2,1,0:T(8,128)(2,1)S(1)}, u32[]{:S(2)}, u32[]{:S(2)}) collective-permute-start(bf16[6,8,16,256]{3,2,1,0:T(8,128)(2,1)S(1)} %join.19.refs_1_), channel_id=1, source_target_pairs={{0,8},{8,24},{24,16},{16,0},{1,9},{9,25},{25,17},{17,1},{2,10},{10... | collective-permute-start | bytes 1179656 | tf_op jit(solution)/shard_map/ppermute | solution.py:268
  72.4 0.7 collective-permute-start.9
  73.2 0.9 turn.4.left_ref
  74.0 1.7 %collective-permute-done.22.refs_8_ = bf16[3,8,16,256]{3,2,1,0:T(8,128)(2,1)S(1)} collective-permute-done((bf16[3,8,16,256]{3,2,1,0:T(8,128)(2,1)S(1)}, bf16[3,8,16,256]{3,2,1,0:T(8,128)(2,1)S(1)}, u32[]{:S(2)}, u32[]{:S(2)}) %collective-permute-start.22) | collective-permute-done | bytes 196640 | tf_op jit(solution)/shard_map/ppermute | solution.py:282
  75.7 1.3 %collective-permute-done.23.refs_9_ = bf16[3,8,16,256]{3,2,1,0:T(8,128)(2,1)S(1)} collective-permute-done((bf16[3,8,16,256]{3,2,1,0:T(8,128)(2,1)S(1)}, bf16[3,8,16,256]{3,2,1,0:T(8,128)(2,1)S(1)}, u32[]{:S(2)}, u32[]{:S(2)}) %collective-permute-start.23) | collective-permute-done | bytes 196640 | tf_op jit(solution)/shard_map/ppermute | solution.py:283
  77.0 7.9 %stack.4.refs_10_ = bf16[48,2,256,1024]{3,2,1,0:T(8,128)(2,1)} custom-call(bf16[8,2,2,256,128]{4,3,2,1,0:T(8,128)(2,1)S(1)} %turn.4.left_ref, bf16[2,24,16,256]{3,2,1,0:T(8,128)(2,1)S(1)} %join.13.refs_0_, bf16[6,8,16,256]{3,2,1,0:T(8,128)(2,1)S(1)} %join.22.refs_1_, ...), custom_call_target="tpu_custom_call", output_to_operand_aliasing={{}: (11, {})} | custom-call | flops 2147483648 | bytes 16777216 | tf_op jit(solution)/shard_map/stack/pallas_call | solution.py:236
  84.9 0.0 collective-permute-done.8.refs_3_
  84.9 0.0 collective-permute-done.9.refs_5_
  84.9 0.7 collective-permute-start.24
  85.6 1.4 %collective-permute-start.25 = (bf16[3,8,16,256]{3,2,1,0:T(8,128)(2,1)S(1)}, bf16[3,8,16,256]{3,2,1,0:T(8,128)(2,1)S(1)}, u32[]{:S(2)}, u32[]{:S(2)}) collective-permute-start(bf16[3,8,16,256]{3,2,1,0:T(8,128)(2,1)S(1)} %slice.31), channel_id=1, source_target_pairs={{8,0},{24,8},{16,24},{0,16},{9,1},{25,9},{17,25},{1,17},{10,2},{26... | collective-permute-start | bytes 589832 | tf_op jit(solution)/shard_map/ppermute | solution.py:283
  87.0 0.9 turn.3.left_ref
  87.9 2.7 %collective-permute-done.24.refs_8_ = bf16[3,8,16,256]{3,2,1,0:T(8,128)(2,1)S(1)} collective-permute-done((bf16[3,8,16,256]{3,2,1,0:T(8,128)(2,1)S(1)}, bf16[3,8,16,256]{3,2,1,0:T(8,128)(2,1)S(1)}, u32[]{:S(2)}, u32[]{:S(2)}) %collective-permute-start.24) | collective-permute-done | bytes 196640 | tf_op jit(solution)/shard_map/ppermute | solution.py:282
  90.6 0.7 collective-permute-done.25.refs_9_
  91.3 7.9 %stack.5 = bf16[48,2,256,1024]{3,2,1,0:T(8,128)(2,1)} custom-call(bf16[8,2,2,256,128]{4,3,2,1,0:T(8,128)(2,1)S(1)} %turn.3.left_ref, bf16[2,24,16,256]{3,2,1,0:T(8,128)(2,1)S(1)} %join.13.refs_0_, bf16[6,8,16,256]{3,2,1,0:T(8,128)(2,1)S(1)} %join.19.refs_1_, ...), custom_call_target="tpu_custom_call", output_to_operand_aliasing={{}: (11, {})} | custom-call | flops 2147483648 | bytes 16777216 | tf_op jit(solution)/shard_map/stack/pallas_call | solution.py:236
  (21 shorter events, 0.3 us)
Async XLA Ops:
  0.0 0.7 copy-start
  0.7 0.7 copy-start.1
  15.7 2.4 %collective-permute-start = (bf16[4,24,16,256]{3,2,1,0:T(8,128)(2,1)S(1)}, bf16[4,24,16,256]{3,2,1,0:T(8,128)(2,1)S(1)}, u32[]{:S(2)}, u32[]{:S(2)}) collective-permute-start(bf16[4,24,16,256]{3,2,1,0:T(8,128)(2,1)S(1)} %get-tuple-element.18), channel_id=1, source_target_pairs={{0,1},{1,0},{2,3},{3,2},{4,5},{5,4},{6,7},{7,6},{8,9},{9,8},{10,11... | collective-permute-start | bytes 2359304 | tf_op jit(solution)/shard_map/ppermute | solution.py:311
  18.1 8.6 %collective-permute-start.3 = (bf16[2,8,16,256]{3,2,1,0:T(8,128)(2,1)S(1)}, bf16[2,8,16,256]{3,2,1,0:T(8,128)(2,1)S(1)}, u32[]{:S(2)}, u32[]{:S(2)}) collective-permute-start(bf16[2,8,16,256]{3,2,1,0:T(8,128)(2,1)S(1)} %join.16), channel_id=1, source_target_pairs={{0,2},{1,3},{2,0},{3,1},{4,6},{5,7},{6,4},{7,5},{8,10},{9,11},{10,... | collective-permute-start | bytes 393224 | tf_op jit(solution)/shard_map/ppermute | solution.py:323
  21.1 13.0 %collective-permute-start.16 = (bf16[2,8,16,256]{3,2,1,0:T(8,128)(2,1)S(1)}, bf16[2,8,16,256]{3,2,1,0:T(8,128)(2,1)S(1)}, u32[]{:S(2)}, u32[]{:S(2)}) collective-permute-start(bf16[2,8,16,256]{3,2,1,0:T(8,128)(2,1)S(1)} %join.23), channel_id=1, source_target_pairs={{0,4},{1,5},{2,6},{3,7},{4,0},{5,1},{6,2},{7,3},{8,12},{9,13},{10,... | collective-permute-start | bytes 393224 | tf_op jit(solution)/shard_map/ppermute | solution.py:323
  23.8 10.3 %collective-permute-start.17 = (bf16[2,8,16,256]{3,2,1,0:T(8,128)(2,1)S(1)}, bf16[2,8,16,256]{3,2,1,0:T(8,128)(2,1)S(1)}, u32[]{:S(2)}, u32[]{:S(2)}) collective-permute-start(bf16[2,8,16,256]{3,2,1,0:T(8,128)(2,1)S(1)} %join.24), channel_id=1, source_target_pairs={{0,6},{1,7},{2,4},{3,5},{4,2},{5,3},{6,0},{7,1},{8,14},{9,15},{10,... | collective-permute-start | bytes 393224 | tf_op jit(solution)/shard_map/ppermute | solution.py:323
  23.9 12.3 %collective-permute-start.1 = (bf16[2,24,16,256]{3,2,1,0:T(8,128)(2,1)S(1)}, bf16[2,24,16,256]{3,2,1,0:T(8,128)(2,1)S(1)}, u32[]{:S(2)}, u32[]{:S(2)}) collective-permute-start(bf16[2,24,16,256]{3,2,1,0:T(8,128)(2,1)S(1)} %join.13.refs_0_), channel_id=1, source_target_pairs={{0,8},{8,24},{24,16},{16,0},{1,9},{9,25},{25,17},{17,1},{2,10},{10... | collective-permute-start | bytes 1179656 | tf_op jit(solution)/shard_map/ppermute | solution.py:268
  25.7 12.1 %collective-permute-start.2 = (bf16[2,24,16,256]{3,2,1,0:T(8,128)(2,1)S(1)}, bf16[2,24,16,256]{3,2,1,0:T(8,128)(2,1)S(1)}, u32[]{:S(2)}, u32[]{:S(2)}) collective-permute-start(bf16[2,24,16,256]{3,2,1,0:T(8,128)(2,1)S(1)} %join.13.refs_0_), channel_id=1, source_target_pairs={{8,0},{24,8},{16,24},{0,16},{9,1},{25,9},{17,25},{1,17},{10,2},{26... | collective-permute-start | bytes 1179656 | tf_op jit(solution)/shard_map/ppermute | solution.py:269
  34.1 11.2 %collective-permute-start.18 = (bf16[6,8,16,256]{3,2,1,0:T(8,128)(2,1)S(1)}, bf16[6,8,16,256]{3,2,1,0:T(8,128)(2,1)S(1)}, u32[]{:S(2)}, u32[]{:S(2)}) collective-permute-start(bf16[6,8,16,256]{3,2,1,0:T(8,128)(2,1)S(1)} %join.25.refs_1_), channel_id=1, source_target_pairs={{0,8},{8,24},{24,16},{16,0},{1,9},{9,25},{25,17},{17,1},{2,10},{10... | collective-permute-start | bytes 1179656 | tf_op jit(solution)/shard_map/ppermute | solution.py:268
  35.7 12.9 %collective-permute-start.19 = (bf16[6,8,16,256]{3,2,1,0:T(8,128)(2,1)S(1)}, bf16[6,8,16,256]{3,2,1,0:T(8,128)(2,1)S(1)}, u32[]{:S(2)}, u32[]{:S(2)}) collective-permute-start(bf16[6,8,16,256]{3,2,1,0:T(8,128)(2,1)S(1)} %join.25.refs_1_), channel_id=1, source_target_pairs={{8,0},{24,8},{16,24},{0,16},{9,1},{25,9},{17,25},{1,17},{10,2},{26... | collective-permute-start | bytes 1179656 | tf_op jit(solution)/shard_map/ppermute | solution.py:269
  36.2 17.4 %collective-permute-start.10 = (bf16[1,24,16,256]{3,2,1,0:T(8,128)(2,1)S(1)}, bf16[1,24,16,256]{3,2,1,0:T(8,128)(2,1)S(1)}, u32[]{:S(2)}, u32[]{:S(2)}) collective-permute-start(bf16[1,24,16,256]{3,2,1,0:T(8,128)(2,1)S(1)} %slice.32), channel_id=1, source_target_pairs={{0,8},{8,24},{24,16},{16,0},{1,9},{9,25},{25,17},{17,1},{2,10},{10... | collective-permute-start | bytes 589832 | tf_op jit(solution)/shard_map/ppermute | solution.py:282
  37.8 12.3 %collective-permute-start.13 = (bf16[2,8,16,256]{3,2,1,0:T(8,128)(2,1)S(1)}, bf16[2,8,16,256]{3,2,1,0:T(8,128)(2,1)S(1)}, u32[]{:S(2)}, u32[]{:S(2)}) collective-permute-start(bf16[2,8,16,256]{3,2,1,0:T(8,128)(2,1)S(1)} %join.21), channel_id=1, source_target_pairs={{0,6},{1,7},{2,4},{3,5},{4,2},{5,3},{6,0},{7,1},{8,14},{9,15},{10,... | collective-permute-start | bytes 393224 | tf_op jit(solution)/shard_map/ppermute | solution.py:323
  40.6 10.2 %collective-permute-start.12 = (bf16[2,8,16,256]{3,2,1,0:T(8,128)(2,1)S(1)}, bf16[2,8,16,256]{3,2,1,0:T(8,128)(2,1)S(1)}, u32[]{:S(2)}, u32[]{:S(2)}) collective-permute-start(bf16[2,8,16,256]{3,2,1,0:T(8,128)(2,1)S(1)} %join.20), channel_id=1, source_target_pairs={{0,4},{1,5},{2,6},{3,7},{4,0},{5,1},{6,2},{7,3},{8,12},{9,13},{10,... | collective-permute-start | bytes 393224 | tf_op jit(solution)/shard_map/ppermute | solution.py:323
  45.3 7.0 %collective-permute-start.4 = (bf16[2,8,16,256]{3,2,1,0:T(8,128)(2,1)S(1)}, bf16[2,8,16,256]{3,2,1,0:T(8,128)(2,1)S(1)}, u32[]{:S(2)}, u32[]{:S(2)}) collective-permute-start(bf16[2,8,16,256]{3,2,1,0:T(8,128)(2,1)S(1)} %join.15), channel_id=1, source_target_pairs={{0,2},{1,3},{2,0},{3,1},{4,6},{5,7},{6,4},{7,5},{8,10},{9,11},{10,... | collective-permute-start | bytes 393224 | tf_op jit(solution)/shard_map/ppermute | solution.py:323
  48.6 7.8 %collective-permute-start.11 = (bf16[1,24,16,256]{3,2,1,0:T(8,128)(2,1)S(1)}, bf16[1,24,16,256]{3,2,1,0:T(8,128)(2,1)S(1)}, u32[]{:S(2)}, u32[]{:S(2)}) collective-permute-start(bf16[1,24,16,256]{3,2,1,0:T(8,128)(2,1)S(1)} %slice.33), channel_id=1, source_target_pairs={{8,0},{24,8},{16,24},{0,16},{9,1},{25,9},{17,25},{1,17},{10,2},{26... | collective-permute-start | bytes 589832 | tf_op jit(solution)/shard_map/ppermute | solution.py:283
  50.2 7.9 %collective-permute-start.20 = (bf16[3,8,16,256]{3,2,1,0:T(8,128)(2,1)S(1)}, bf16[3,8,16,256]{3,2,1,0:T(8,128)(2,1)S(1)}, u32[]{:S(2)}, u32[]{:S(2)}) collective-permute-start(bf16[3,8,16,256]{3,2,1,0:T(8,128)(2,1)S(1)} %slice.34), channel_id=1, source_target_pairs={{0,8},{8,24},{24,16},{16,0},{1,9},{9,25},{25,17},{17,1},{2,10},{10... | collective-permute-start | bytes 589832 | tf_op jit(solution)/shard_map/ppermute | solution.py:282
  50.7 9.9 %collective-permute-start.21 = (bf16[3,8,16,256]{3,2,1,0:T(8,128)(2,1)S(1)}, bf16[3,8,16,256]{3,2,1,0:T(8,128)(2,1)S(1)}, u32[]{:S(2)}, u32[]{:S(2)}) collective-permute-start(bf16[3,8,16,256]{3,2,1,0:T(8,128)(2,1)S(1)} %slice.35), channel_id=1, source_target_pairs={{8,0},{24,8},{16,24},{0,16},{9,1},{25,9},{17,25},{1,17},{10,2},{26... | collective-permute-start | bytes 589832 | tf_op jit(solution)/shard_map/ppermute | solution.py:283
  52.3 16.5 %collective-permute-start.14 = (bf16[6,8,16,256]{3,2,1,0:T(8,128)(2,1)S(1)}, bf16[6,8,16,256]{3,2,1,0:T(8,128)(2,1)S(1)}, u32[]{:S(2)}, u32[]{:S(2)}) collective-permute-start(bf16[6,8,16,256]{3,2,1,0:T(8,128)(2,1)S(1)} %join.22.refs_1_), channel_id=1, source_target_pairs={{0,8},{8,24},{24,16},{16,0},{1,9},{9,25},{25,17},{17,1},{2,10},{10... | collective-permute-start | bytes 1179656 | tf_op jit(solution)/shard_map/ppermute | solution.py:268
  53.7 15.2 %collective-permute-start.15 = (bf16[6,8,16,256]{3,2,1,0:T(8,128)(2,1)S(1)}, bf16[6,8,16,256]{3,2,1,0:T(8,128)(2,1)S(1)}, u32[]{:S(2)}, u32[]{:S(2)}) collective-permute-start(bf16[6,8,16,256]{3,2,1,0:T(8,128)(2,1)S(1)} %join.22.refs_1_), channel_id=1, source_target_pairs={{8,0},{24,8},{16,24},{0,16},{9,1},{25,9},{17,25},{1,17},{10,2},{26... | collective-permute-start | bytes 1179656 | tf_op jit(solution)/shard_map/ppermute | solution.py:269
  56.4 14.6 %collective-permute-start.7 = (bf16[2,8,16,256]{3,2,1,0:T(8,128)(2,1)S(1)}, bf16[2,8,16,256]{3,2,1,0:T(8,128)(2,1)S(1)}, u32[]{:S(2)}, u32[]{:S(2)}) collective-permute-start(bf16[2,8,16,256]{3,2,1,0:T(8,128)(2,1)S(1)} %join.18), channel_id=1, source_target_pairs={{0,6},{1,7},{2,4},{3,5},{4,2},{5,3},{6,0},{7,1},{8,14},{9,15},{10,... | collective-permute-start | bytes 393224 | tf_op jit(solution)/shard_map/ppermute | solution.py:323
  58.1 13.0 %collective-permute-start.6 = (bf16[2,8,16,256]{3,2,1,0:T(8,128)(2,1)S(1)}, bf16[2,8,16,256]{3,2,1,0:T(8,128)(2,1)S(1)}, u32[]{:S(2)}, u32[]{:S(2)}) collective-permute-start(bf16[2,8,16,256]{3,2,1,0:T(8,128)(2,1)S(1)} %join.17), channel_id=1, source_target_pairs={{0,4},{1,5},{2,6},{3,7},{4,0},{5,1},{6,2},{7,3},{8,12},{9,13},{10,... | collective-permute-start | bytes 393224 | tf_op jit(solution)/shard_map/ppermute | solution.py:323
  60.6 10.4 %collective-permute-start.5 = (bf16[2,8,16,256]{3,2,1,0:T(8,128)(2,1)S(1)}, bf16[2,8,16,256]{3,2,1,0:T(8,128)(2,1)S(1)}, u32[]{:S(2)}, u32[]{:S(2)}) collective-permute-start(bf16[2,8,16,256]{3,2,1,0:T(8,128)(2,1)S(1)} %join.14), channel_id=1, source_target_pairs={{0,2},{1,3},{2,0},{3,1},{4,6},{5,7},{6,4},{7,5},{8,10},{9,11},{10,... | collective-permute-start | bytes 393224 | tf_op jit(solution)/shard_map/ppermute | solution.py:323
  68.9 6.8 %collective-permute-start.22 = (bf16[3,8,16,256]{3,2,1,0:T(8,128)(2,1)S(1)}, bf16[3,8,16,256]{3,2,1,0:T(8,128)(2,1)S(1)}, u32[]{:S(2)}, u32[]{:S(2)}) collective-permute-start(bf16[3,8,16,256]{3,2,1,0:T(8,128)(2,1)S(1)} %slice.28), channel_id=1, source_target_pairs={{0,8},{8,24},{24,16},{16,0},{1,9},{9,25},{25,17},{17,1},{2,10},{10... | collective-permute-start | bytes 589832 | tf_op jit(solution)/shard_map/ppermute | solution.py:282
  70.2 6.7 %collective-permute-start.23 = (bf16[3,8,16,256]{3,2,1,0:T(8,128)(2,1)S(1)}, bf16[3,8,16,256]{3,2,1,0:T(8,128)(2,1)S(1)}, u32[]{:S(2)}, u32[]{:S(2)}) collective-permute-start(bf16[3,8,16,256]{3,2,1,0:T(8,128)(2,1)S(1)} %slice.29), channel_id=1, source_target_pairs={{8,0},{24,8},{16,24},{0,16},{9,1},{25,9},{17,25},{1,17},{10,2},{26... | collective-permute-start | bytes 589832 | tf_op jit(solution)/shard_map/ppermute | solution.py:283
  71.1 13.8 %collective-permute-start.8 = (bf16[6,8,16,256]{3,2,1,0:T(8,128)(2,1)S(1)}, bf16[6,8,16,256]{3,2,1,0:T(8,128)(2,1)S(1)}, u32[]{:S(2)}, u32[]{:S(2)}) collective-permute-start(bf16[6,8,16,256]{3,2,1,0:T(8,128)(2,1)S(1)} %join.19.refs_1_), channel_id=1, source_target_pairs={{0,8},{8,24},{24,16},{16,0},{1,9},{9,25},{25,17},{17,1},{2,10},{10... | collective-permute-start | bytes 1179656 | tf_op jit(solution)/shard_map/ppermute | solution.py:268
  72.4 12.5 %collective-permute-start.9 = (bf16[6,8,16,256]{3,2,1,0:T(8,128)(2,1)S(1)}, bf16[6,8,16,256]{3,2,1,0:T(8,128)(2,1)S(1)}, u32[]{:S(2)}, u32[]{:S(2)}) collective-permute-start(bf16[6,8,16,256]{3,2,1,0:T(8,128)(2,1)S(1)} %join.19.refs_1_), channel_id=1, source_target_pairs={{8,0},{24,8},{16,24},{0,16},{9,1},{25,9},{17,25},{1,17},{10,2},{26... | collective-permute-start | bytes 1179656 | tf_op jit(solution)/shard_map/ppermute | solution.py:269
  84.9 5.7 %collective-permute-start.24 = (bf16[3,8,16,256]{3,2,1,0:T(8,128)(2,1)S(1)}, bf16[3,8,16,256]{3,2,1,0:T(8,128)(2,1)S(1)}, u32[]{:S(2)}, u32[]{:S(2)}) collective-permute-start(bf16[3,8,16,256]{3,2,1,0:T(8,128)(2,1)S(1)} %slice.30), channel_id=1, source_target_pairs={{0,8},{8,24},{24,16},{16,0},{1,9},{9,25},{25,17},{17,1},{2,10},{10... | collective-permute-start | bytes 589832 | tf_op jit(solution)/shard_map/ppermute | solution.py:282
  85.6 5.7 %collective-permute-start.25 = (bf16[3,8,16,256]{3,2,1,0:T(8,128)(2,1)S(1)}, bf16[3,8,16,256]{3,2,1,0:T(8,128)(2,1)S(1)}, u32[]{:S(2)}, u32[]{:S(2)}) collective-permute-start(bf16[3,8,16,256]{3,2,1,0:T(8,128)(2,1)S(1)} %slice.31), channel_id=1, source_target_pairs={{8,0},{24,8},{16,24},{0,16},{9,1},{25,9},{17,25},{1,17},{10,2},{26... | collective-permute-start | bytes 589832 | tf_op jit(solution)/shard_map/ppermute | solution.py:283

commit v2 on v1

--- a/solution.py
+++ b/solution.py
@@ -34,7 +34,8 @@
     rows = 2 * windows * bins
     row = lax.broadcasted_iota(jnp.int32, (rows, rows), 0)
     col = lax.broadcasted_iota(jnp.int32, (rows, rows), 1)
-    w, b, p, g = row % windows, row // windows % pair, row // 8 % 2, row // 16
+    w, p = row & (windows - 1), (row >> 3) & 1
+    b, g = (row & 7) >> (windows.bit_length() - 1), row >> 4
     return jnp.where(col == (w * 2 + p) * bins + g * pair + b, 1.0, 0.0).astype(jnp.bfloat16)
 
 
@@ -59,24 +60,25 @@
         window_ref[step * tile : (step + 1) * tile, :] = moved.reshape(tile, width).astype(jnp.bfloat16)
 
 
-def spectra_kernel(offsets_ref, table_hbm, raw_hbm, quality_hbm, keep_ref, give_ref, *scratch):
+def spectra_kernel(chips, offsets_ref, table_hbm, raw_hbm, quality_hbm, keep_ref, give_ref, *scratch):
     table_ref, quality_ref, raw_ref, white, mixed, sems = scratch[:6]
     cuts = scratch[6:]
     windows, _, width = raw_ref.shape
     loads = [pltpu.make_async_copy(raw_hbm.at[w], raw_ref.at[w], sems.at[w]) for w in range(windows)]
     table_load = pltpu.make_async_copy(table_hbm, table_ref, sems.at[windows])
     quality_load = pltpu.make_async_copy(quality_hbm, quality_ref, sems.at[windows + 1])
-    for load in (loads[0], quality_load, table_load, *loads[1:]):
+    early = min(2, windows)
+    for load in (*loads[:early], table_load, *loads[early:], quality_load):
         load.start()
-    loads[0].wait()
-    cut(raw_ref, 0, offsets_ref[0], cuts[0])
     mix = interleave(windows, 256 // (2 * windows))
-    quality_load.wait()
-    table_load.wait()
+    for w in range(early):
+        loads[w].wait()
+        cut(raw_ref, w, offsets_ref[w], cuts[w])
+    for load in (table_load, *loads[early:], quality_load):
+        load.wait()
     for w in range(windows):
-        if w + 1 < windows:
-            loads[w + 1].wait()
-            cut(raw_ref, w + 1, offsets_ref[w + 1], cuts[w + 1])
+        if w + early < windows:
+            cut(raw_ref, w + early, offsets_ref[w + early], cuts[w + early])
         transform = jnp.dot(table_ref[...], cuts[w][...], preferred_element_type=jnp.float32)
         band_power = jnp.sum(transform * transform, axis=0, keepdims=True) / F
         usable = quality_ref[w : w + 1, :].astype(jnp.float32)
@@ -93,11 +95,11 @@
         mixed[block * groups : (block + 1) * groups] = product.astype(jnp.bfloat16).reshape(groups, 16, width)
     me = lax.axis_index("win")
     chip, core = me // 2, me % 2
-    chips, share = keep_ref.shape[:2]
+    share = keep_ref.shape[0] // chips
     for k in range(chips):
         at = (chip ^ k) * 2 * share
-        keep_ref[k] = mixed[pl.ds(at + core * share, share)]
-        give_ref[k] = mixed[pl.ds(at + (1 - core) * share, share)]
+        keep_ref[k * share : (k + 1) * share] = mixed[pl.ds(at + core * share, share)]
+        give_ref[k * share : (k + 1) * share] = mixed[pl.ds(at + (1 - core) * share, share)]
 
 
 def in_vmem(count):
@@ -107,9 +109,9 @@
 def spectra(raw, offsets, quality, table, dests):
     windows, _, width = raw.shape
     groups = F * 2 * windows // 16
-    blocks = (dests // 2, groups // dests, 16, width)
+    blocks = (groups // 2, 16, width)
     return pl.pallas_call(
-        spectra_kernel,
+        functools.partial(spectra_kernel, dests // 2),
         in_specs=[pl.BlockSpec(memory_space=pltpu.SMEM)] + [pl.BlockSpec(memory_space=pl.ANY)] * 3,
         out_specs=in_vmem(2),
         scratch_shapes=[
@@ -130,24 +132,30 @@
     )(offsets, table, raw, quality)
 
 
+def part_of(view, low, high):
+    x, base, _, groups, first = view
+    return (x, base + low * groups, high - low, groups, first)
+
+
 def join_kernel(moves, *refs):
     out_ref = refs[-1]
-    groups = out_ref.shape[1]
     to = 0
-    for i, at, source, count in moves:
-        out_ref[to : to + count] = refs[i][source : source + count, at : at + groups]
+    for i, at, count in moves:
+        out_ref[to : to + count] = refs[i][at : at + count]
         to += count
 
 
-def join(views, groups):
-    arrays, moves = [], []
-    for x, *where in views:
+def join(views):
+    arrays, moves, places, to = [], [], [], 0
+    for x, base, sources, groups, first in views:
         known = [i for i, y in enumerate(arrays) if y is x]
         if not known:
             arrays.append(x)
-        moves.append((known[0] if known else len(arrays) - 1, *where))
-    shape = (sum(move[3] for move in moves), groups, *arrays[0].shape[2:])
-    return pl.pallas_call(
+        moves.append((known[0] if known else len(arrays) - 1, base, sources * groups))
+        places.append((to, sources, groups, first))
+        to += sources * groups
+    shape = (to, *arrays[0].shape[1:])
+    joined = pl.pallas_call(
         functools.partial(join_kernel, moves),
         in_specs=in_vmem(len(arrays)),
         out_specs=in_vmem(1)[0],
@@ -156,10 +164,22 @@
         cost_estimate=pl.CostEstimate(flops=0, bytes_accessed=4 * math.prod(shape), transcendentals=0),
         name="join",
     )(*arrays)
-
-
-def view(ref, group, at, sources):
-    return ref[sources[0] : sources[1], group - at].reshape(-1, ref.shape[-1])
+    return joined, places
+
+
+def gathered(ref, group, place):
+    base, sources, groups, first = place
+    return [ref[base + source * groups + group - first] for source in range(sources)]
+
+
+def operands_of(views):
+    arrays, places = [], []
+    for x, *place in views:
+        known = [i for i, y in enumerate(arrays) if y is x]
+        if not known:
+            arrays.append(x)
+        places.append((known[0] if known else len(arrays) - 1, place))
+    return arrays, places
 
 
 def turn_kernel(windows, first_group, views, *refs):
@@ -168,7 +188,7 @@
     bin_of = lax.broadcasted_iota(jnp.int32, (width, depth), 1) % 8 // windows
 
     def body(g, carry):
-        x = jnp.concatenate([view(refs[i], first_group + g, *where) for i, where in enumerate(views)], 0)
+        x = jnp.concatenate(sum([gathered(refs[i], first_group + g, place) for i, place in views], []), 0)
         by_part = x.astype(jnp.float32).reshape(depth // 16, 16, width)
         turned = jnp.concatenate([by_part[:, 8:], -by_part[:, :8]], 1)
         for part, rows in enumerate((by_part, turned)):
@@ -180,19 +200,20 @@
     lax.fori_loop(0, out_ref.shape[0], body, 0)
 
 
-def turn(items, first_group, groups, windows):
-    rows, width = items[0][0].shape[2:]
-    depth = sum(sources[1] - sources[0] for _, _, sources in items) * rows
+def turn(views, first_group, groups, windows):
+    arrays, places = operands_of(views)
+    rows, width = arrays[0].shape[1:]
+    depth = sum(place[1] for _, place in places) * rows
     pair = 16 // (2 * windows)
     return pl.pallas_call(
-        functools.partial(turn_kernel, windows, first_group, [item[1:] for item in items]),
-        in_specs=in_vmem(len(items)),
+        functools.partial(turn_kernel, windows, first_group, places),
+        in_specs=in_vmem(len(arrays)),
         out_specs=in_vmem(1)[0],
         out_shape=jax.ShapeDtypeStruct((groups, pair, 2, width, depth), jnp.bfloat16),
         compiler_params=pltpu.CompilerParams(vmem_limit_bytes=12 * MIB),
         cost_estimate=pl.CostEstimate(flops=0, bytes_accessed=8 * groups * width * depth, transcendentals=0),
         name="turn",
-    )(*[item[0] for item in items])
+    )(*arrays)
 
 
 def closed_walk(i, members):
@@ -208,7 +229,7 @@
     for s in range(step_groups):
         g = pl.program_id(0) * step_groups + s
         for step, items in layout:
-            right = jnp.concatenate([view(refs[i], first_group + g, *item) for i, item in items], 0)
+            right = jnp.concatenate(sum([gathered(refs[i], first_group + g, place) for i, place in items], []), 0)
             column = closed_walk(lax.rem(where + (step + members), members), members)
             columns = pl.ds(pl.multiple_of(column * width, width), width)
             for b in range(pair):
@@ -222,10 +243,12 @@
     members = len(steps)
     _, pair, _, width, depth = left.shape
     step_groups = max(n for n in range(1, STEP_GROUPS + 1) if groups % n == 0 and first_group % n == 0)
-    operands, layout = [left], []
-    for step, items in steps:
-        layout.append((step, [(len(operands) - 1 + i, item[1:]) for i, item in enumerate(items)]))
-        operands += [item[0] for item in items]
+    arrays, places = operands_of(sum([views for _, views in steps], []))
+    layout = []
+    for step, views in steps:
+        layout.append((step, places[: len(views)]))
+        places = places[len(views) :]
+    operands = [left, *arrays]
     in_specs = in_vmem(len(operands))
     aliases = {}
     if into is not None:
@@ -259,33 +282,28 @@
     return [(ring[i], ring[(i + 1) % members]) for i in range(members)]
 
 
-def ring_start(x, members):
+def halves_of(views, total):
+    first, second, seen = [], [], 0
+    for view in views:
+        cut_at = min(max(total // 2 - seen, 0), view[2])
+        first += [part_of(view, 0, cut_at)] if cut_at else []
+        second += [part_of(view, cut_at, view[2])] if cut_at < view[2] else []
+        seen += view[2]
+    return first, second
+
+
+def ring_phase(travellers, members):
     ahead = ring_walk(members)
-    back = [(b, a) for a, b in ahead]
-    left = right = x
-    blocks = [(0, [x])]
-    for step in range(1, (members + 1) // 2):
-        left = lax.ppermute(left, "chan", ahead)
-        right = lax.ppermute(right, "chan", back)
-        blocks += [(-step, [left]), (step, [right])]
-    return blocks
-
-
-def ring_finish(blocks, members, *earlier):
-    if members % 2:
-        return blocks
-    ahead = ring_walk(members)
-    left, right = blocks[-2][1][0], blocks[-1][1][0]
-    if earlier:
-        left, right = after((left, right), *earlier)
-    cut_at = left.shape[0] // 2
-    first = lax.ppermute(left[:cut_at], "chan", ahead)
-    second = lax.ppermute(right[cut_at:], "chan", [(b, a) for a, b in ahead])
-    return blocks + [(members // 2, [first, second])]
-
-
-def neighbours(blocks):
-    return [array for step, arrays in blocks if step for array in arrays]
+    moved = []
+    for way, pairs in ((0, ahead), (1, [(b, a) for a, b in ahead])):
+        sent, places = join(sum([views[way] for views in travellers], []))
+        came = lax.ppermute(sent, "chan", pairs)
+        moved.append([(came, *place) for place in places])
+    result = []
+    for views in travellers:
+        result.append((moved[0][: len(views[0])], moved[1][: len(views[1])]))
+        moved = [moved[0][len(views[0]) :], moved[1][len(views[1]) :]]
+    return result
 
 
 def chunk_starts(share):
@@ -309,31 +327,52 @@
 
     keep, give = spectra(raw, offsets, quality, table, dests)
     other = lax.ppermute(give, "win", [(i, i ^ 1) for i in range(dests)])
-    own = join([(keep, 0, 0, 1), (other, 0, 0, 1)], share)
-    own_start = ring_start(own, members)
-    own_blocks = ring_finish(own_start, members)
-
-    pieces = []
-    for start, stop in chunks:
+    def travel(n, *earlier):
+        start, stop = chunks[n]
         came = []
         for k in range(1, chips):
-            sent = join([(keep, start, k, 1), (other, start, k, 1)], stop - start)
-            if pieces:
-                sent = after([sent], *neighbours(own_start), pieces[-1][0])[0]
+            sent, _ = join([(x, k * share + start, 1, stop - start, start) for x in (keep, other)])
+            if earlier:
+                sent = after([sent], *earlier)[0]
             came.append(lax.ppermute(sent, "win", [(i, i ^ (2 * k)) for i in range(dests)]))
-        pieces.append(came)
-
+        return [(x, 0, 2, stop - start, start) for x in came]
+
+    units = [[(x, 0, 1, share, 0) for x in (keep, other)]]
+    turns = members // 2
+    found = [[(0, units[0])]]
+    held = [(units[0], units[0])]
     out = None
-    for n, ((start, stop), came) in enumerate(zip(chunks, pieces)):
-        far = join([(x, 0, 0, 2) for x in came], stop - start)
-        begun = ring_start(far, members)
-        blocks = ring_finish(begun, members, *([] if out is None else [out]))
-        steps = []
-        for (step, own_arrays), (_, arrays) in zip(own_blocks, blocks):
-            views = [(x, 0, (0, x.shape[0])) for x in own_arrays] + [(x, start, (0, x.shape[0])) for x in arrays]
-            steps.append((step, views))
-        left = turn(steps[0][1], start, stop - start, windows)
-        out = stack(left, start, steps, out, start, stop - start, bins, dests * windows)
+    stacked = 0
+    for phase in range(len(chunks) + turns):
+        travellers, who = [], []
+        for u in range(len(units)):
+            step = phase - u + 1
+            if not 1 <= step <= turns:
+                continue
+            left, right = held[u]
+            if step == turns:
+                total = sum(view[2] for view in left)
+                left, right = halves_of(left, total)[0], halves_of(right, total)[1]
+            travellers.append((left, right))
+            who.append((u, step))
+        if phase < len(chunks):
+            arrives = travel(phase, *([x[0] for x in units[-1][:1]] if phase else []))
+        for (u, step), (left, right) in zip(who, ring_phase(travellers, members)):
+            held[u] = (left, right)
+            if step == turns:
+                found[u].append((turns, left + right))
+            else:
+                found[u] += [(-step, left), (step, right)]
+        if phase < len(chunks):
+            units.append(arrives)
+            held.append((arrives, arrives))
+            found.append([(0, arrives)])
+        while stacked < phase - turns or (phase + 1 == len(chunks) + turns and stacked < len(chunks)):
+            start, stop = chunks[stacked]
+            steps = [(a[0], a[1] + b[1]) for a, b in zip(found[0], found[stacked + 1])]
+            left = turn(steps[0][1], start, stop - start, windows)
+            out = stack(left, start, steps, out, start, stop - start, bins, dests * windows)
+            stacked += 1
     return out
 
 

time: 99.4 us -> 93.5 us (0.941)
  starting transfers between devices: 34.1 us -> 25.8 us
  waiting for transfers between devices: 22.6 us -> 28.6 us
  Pallas kernels: 40.8 us -> 37.5 us
    ppermute x25 -> x19, starting transfers between devices: 33.6 us -> 25.3 us  [the longest x9 13.8 us: travel(): lax.ppermute(sent, 'win', [(i, i ^ 2 * k) for i in range(dests)])]
    ppermute x25 -> x19, waiting for transfers between devices: 20.7 us -> 26.7 us  [the longest x9 26.6 us: travel(): lax.ppermute(sent, 'win', [(i, i ^ 2 * k) for i in range(dests)])]
    pallas_call x4, Pallas kernels: 16.9 us -> 13.4 us  [the longest x1 10.8 us: spectra(): pl.pallas_call(functools.partial(spectra_kernel, dests // 2), in_specs=[p...]
  transfers between devices with their start and end apart: 26 -> 20, of which waited for: 10 -> 7; matrix products, arithmetic and copies ran while one was open for 0% -> 0% of each run, Pallas kernels for 19% -> 20%
where the time goes in v2:
time: 93.5 us; the launch traced here: 93.4 us
  Pallas kernels  37.5 us (40%)
  waiting for transfers between devices  28.6 us (31%)
  starting transfers between devices  25.8 us (28%)
  local copies, waits for them, and re-layouts  1.34 us (1%)
    ppermute x9, waiting for transfers between devices, travel(): lax.ppermute(sent, 'win', [(i, i ^ 2 * k) for i in range(dests)])  26.6 us
    pallas_call x3, Pallas kernels, stack(): pl.pallas_call(functools.partial(stack_kernel, 1.0 / math.sqrt(sources),...  23.7 us
    ppermute x9, starting transfers between devices, travel(): lax.ppermute(sent, 'win', [(i, i ^ 2 * k) for i in range(dests)])  13.8 us
    ppermute x10, starting transfers between devices, ring_phase(): came = lax.ppermute(sent, 'chan', pairs)  11.5 us
    pallas_call x1, Pallas kernels, spectra(): pl.pallas_call(functools.partial(spectra_kernel, dests // 2), in_specs=[p...  10.8 us
    pallas_call x3, Pallas kernels, turn(): pl.pallas_call(functools.partial(turn_kernel, windows, first_group, place...  2.59 us
    ppermute x1, waiting for transfers between devices, local(): other = lax.ppermute(give, 'win', [(i, i ^ 1) for i in range(dests)])  1.91 us
  transfers between devices with their start and end apart: 20, of which 7 were waited for; matrix products, arithmetic and copies ran while one was open for 0% of the time, Pallas kernels for 20%

profile of v2, /device:TPU:0, one launch (start us, length us, event | category | flops | bytes accessed | tf_op | source)
XLA Modules:
  0.0 93.4 jit_solution(70574601041634151)
XLA Ops:
  0.0 0.0 copy-start
  0.0 0.7 copy-done
  0.7 0.0 copy-start.1
  0.7 0.7 copy-done.1
  1.3 10.8 %spectra.1 = (bf16[96,16,256]{2,1,0:T(8,128)(2,1)S(1)}, bf16[96,16,256]{2,1,0:T(8,128)(2,1)S(1)}) custom-call(s32[4]{0:T(128)S(1)} %copy-done.1, bf16[768,3072]{1,0:T(8,128)(2,1)} %constant.2.clone.table_hbm, bf16[4,3200,256]{2,1,0:T(8,128)(2,1)} %raw_hbm.1, s32[4,256]{1,0:T(4,128)S(1)} %copy-done), custom_call_target="tpu_custom_call" | custom-call | flops 4831838208 | bytes 11272192 | tf_op jit(solution)/shard_map/spectra/pallas_call | solution.py:113
  12.2 0.5 collective-permute-start
  12.7 1.9 %collective-permute-done.refs_1_ = bf16[96,16,256]{2,1,0:T(8,128)(2,1)S(1)} collective-permute-done((bf16[96,16,256]{2,1,0:T(8,128)(2,1)S(1)}, bf16[96,16,256]{2,1,0:T(8,128)(2,1)S(1)}, u32[]{:S(2)}, u32[]{:S(2)}) %collective-permute-start) | collective-permute-done | bytes 786464 | tf_op jit(solution)/shard_map/ppermute | solution.py:329
  14.6 3.0 %collective-permute-start.14 = (bf16[48,16,256]{2,1,0:T(8,128)(2,1)S(1)}, bf16[48,16,256]{2,1,0:T(8,128)(2,1)S(1)}, u32[]{:S(2)}, u32[]{:S(2)}) collective-permute-start(bf16[48,16,256]{2,1,0:T(8,128)(2,1)S(1)} %join.23), channel_id=1, source_target_pairs={{8,0},{24,8},{16,24},{0,16},{9,1},{25,9},{17,25},{1,17},{10,2},{26... | collective-permute-start | bytes 1179656 | tf_op jit(solution)/shard_map/ppermute | solution.py:300
  17.6 0.0 collective-permute-start.6
  17.6 2.1 %collective-permute-start.1 = (bf16[16,16,256]{2,1,0:T(8,128)(2,1)S(1)}, bf16[16,16,256]{2,1,0:T(8,128)(2,1)S(1)}, u32[]{:S(2)}, u32[]{:S(2)}) collective-permute-start(bf16[16,16,256]{2,1,0:T(8,128)(2,1)S(1)} %join.20), channel_id=1, source_target_pairs={{0,2},{1,3},{2,0},{3,1},{4,6},{5,7},{6,4},{7,5},{8,10},{9,11},{10,... | collective-permute-start | bytes 393224 | tf_op jit(solution)/shard_map/ppermute | solution.py:337
  19.7 2.6 %collective-permute-start.7 = (bf16[16,16,256]{2,1,0:T(8,128)(2,1)S(1)}, bf16[16,16,256]{2,1,0:T(8,128)(2,1)S(1)}, u32[]{:S(2)}, u32[]{:S(2)}) collective-permute-start(bf16[16,16,256]{2,1,0:T(8,128)(2,1)S(1)} %join.24), channel_id=1, source_target_pairs={{0,4},{1,5},{2,6},{3,7},{4,0},{5,1},{6,2},{7,3},{8,12},{9,13},{10,... | collective-permute-start | bytes 393224 | tf_op jit(solution)/shard_map/ppermute | solution.py:337
  22.4 0.1 collective-permute-start.8
  22.5 1.9 %collective-permute-done.1.refs_1_.refs_2_ = bf16[16,16,256]{2,1,0:T(8,128)(2,1)S(1)} collective-permute-done((bf16[16,16,256]{2,1,0:T(8,128)(2,1)S(1)}, bf16[16,16,256]{2,1,0:T(8,128)(2,1)S(1)}, u32[]{:S(2)}, u32[]{:S(2)}) %collective-permute-start.1) | collective-permute-done | bytes 131104 | tf_op jit(solution)/shard_map/ppermute | solution.py:337
  24.3 8.1 %collective-permute-done.7.refs_2_.refs_3_ = bf16[16,16,256]{2,1,0:T(8,128)(2,1)S(1)} collective-permute-done((bf16[16,16,256]{2,1,0:T(8,128)(2,1)S(1)}, bf16[16,16,256]{2,1,0:T(8,128)(2,1)S(1)}, u32[]{:S(2)}, u32[]{:S(2)}) %collective-permute-start.7) | collective-permute-done | bytes 131104 | tf_op jit(solution)/shard_map/ppermute | solution.py:337
  32.4 0.0 collective-permute-done.8.refs_3_.refs_4_
  32.5 0.0 collective-permute-done.14.refs_0_.refs_7_
  32.5 1.6 %collective-permute-start.15 = (bf16[72,16,256]{2,1,0:T(8,128)(2,1)S(1)}, bf16[72,16,256]{2,1,0:T(8,128)(2,1)S(1)}, u32[]{:S(2)}, u32[]{:S(2)}) collective-permute-start(bf16[72,16,256]{2,1,0:T(8,128)(2,1)S(1)} %join.31), channel_id=1, source_target_pairs={{8,0},{24,8},{16,24},{0,16},{9,1},{25,9},{17,25},{1,17},{10,2},{26... | collective-permute-start | bytes 1769480 | tf_op jit(solution)/shard_map/ppermute | solution.py:300
  34.1 0.0 collective-permute-done.6.refs_0_.refs_5_
  34.1 0.6 collective-permute-start.9
  34.7 2.0 %collective-permute-start.2 = (bf16[16,16,256]{2,1,0:T(8,128)(2,1)S(1)}, bf16[16,16,256]{2,1,0:T(8,128)(2,1)S(1)}, u32[]{:S(2)}, u32[]{:S(2)}) collective-permute-start(bf16[16,16,256]{2,1,0:T(8,128)(2,1)S(1)} %join.19), channel_id=1, source_target_pairs={{0,2},{1,3},{2,0},{3,1},{4,6},{5,7},{6,4},{7,5},{8,10},{9,11},{10,... | collective-permute-start | bytes 393224 | tf_op jit(solution)/shard_map/ppermute | solution.py:337
  36.8 1.1 %collective-permute-start.10 = (bf16[16,16,256]{2,1,0:T(8,128)(2,1)S(1)}, bf16[16,16,256]{2,1,0:T(8,128)(2,1)S(1)}, u32[]{:S(2)}, u32[]{:S(2)}) collective-permute-start(bf16[16,16,256]{2,1,0:T(8,128)(2,1)S(1)} %join.27), channel_id=1, source_target_pairs={{0,4},{1,5},{2,6},{3,7},{4,0},{5,1},{6,2},{7,3},{8,12},{9,13},{10,... | collective-permute-start | bytes 393224 | tf_op jit(solution)/shard_map/ppermute | solution.py:337
  37.8 1.4 %collective-permute-start.11 = (bf16[16,16,256]{2,1,0:T(8,128)(2,1)S(1)}, bf16[16,16,256]{2,1,0:T(8,128)(2,1)S(1)}, u32[]{:S(2)}, u32[]{:S(2)}) collective-permute-start(bf16[16,16,256]{2,1,0:T(8,128)(2,1)S(1)} %join.28), channel_id=1, source_target_pairs={{0,6},{1,7},{2,4},{3,5},{4,2},{5,3},{6,0},{7,1},{8,14},{9,15},{10,... | collective-permute-start | bytes 393224 | tf_op jit(solution)/shard_map/ppermute | solution.py:337
  39.2 1.4 %collective-permute-done.2.refs_1_.refs_2_ = bf16[16,16,256]{2,1,0:T(8,128)(2,1)S(1)} collective-permute-done((bf16[16,16,256]{2,1,0:T(8,128)(2,1)S(1)}, bf16[16,16,256]{2,1,0:T(8,128)(2,1)S(1)}, u32[]{:S(2)}, u32[]{:S(2)}) %collective-permute-start.2) | collective-permute-done | bytes 131104 | tf_op jit(solution)/shard_map/ppermute | solution.py:337
  40.6 7.2 %collective-permute-done.10.refs_2_.refs_3_ = bf16[16,16,256]{2,1,0:T(8,128)(2,1)S(1)} collective-permute-done((bf16[16,16,256]{2,1,0:T(8,128)(2,1)S(1)}, bf16[16,16,256]{2,1,0:T(8,128)(2,1)S(1)}, u32[]{:S(2)}, u32[]{:S(2)}) %collective-permute-start.10) | collective-permute-done | bytes 131104 | tf_op jit(solution)/shard_map/ppermute | solution.py:337
  47.8 0.0 collective-permute-done.11.refs_3_.refs_4_
  47.8 0.0 collective-permute-done.15.refs_0_.refs_8_.refs_10_
  47.9 1.6 %collective-permute-start.16 = (bf16[72,16,256]{2,1,0:T(8,128)(2,1)S(1)}, bf16[72,16,256]{2,1,0:T(8,128)(2,1)S(1)}, u32[]{:S(2)}, u32[]{:S(2)}) collective-permute-start(bf16[72,16,256]{2,1,0:T(8,128)(2,1)S(1)} %join.32), channel_id=1, source_target_pairs={{8,0},{24,8},{16,24},{0,16},{9,1},{25,9},{17,25},{1,17},{10,2},{26... | collective-permute-start | bytes 1769480 | tf_op jit(solution)/shard_map/ppermute | solution.py:300
  49.4 0.0 collective-permute-done.9.refs_0_.refs_6_.refs_9_
  49.5 0.6 collective-permute-start.12
  50.1 1.9 %collective-permute-start.5 = (bf16[16,16,256]{2,1,0:T(8,128)(2,1)S(1)}, bf16[16,16,256]{2,1,0:T(8,128)(2,1)S(1)}, u32[]{:S(2)}, u32[]{:S(2)}) collective-permute-start(bf16[16,16,256]{2,1,0:T(8,128)(2,1)S(1)} %join.22), channel_id=1, source_target_pairs={{0,6},{1,7},{2,4},{3,5},{4,2},{5,3},{6,0},{7,1},{8,14},{9,15},{10,... | collective-permute-start | bytes 393224 | tf_op jit(solution)/shard_map/ppermute | solution.py:337
  52.0 1.6 %collective-permute-start.4 = (bf16[16,16,256]{2,1,0:T(8,128)(2,1)S(1)}, bf16[16,16,256]{2,1,0:T(8,128)(2,1)S(1)}, u32[]{:S(2)}, u32[]{:S(2)}) collective-permute-start(bf16[16,16,256]{2,1,0:T(8,128)(2,1)S(1)} %join.21), channel_id=1, source_target_pairs={{0,4},{1,5},{2,6},{3,7},{4,0},{5,1},{6,2},{7,3},{8,12},{9,13},{10,... | collective-permute-start | bytes 393224 | tf_op jit(solution)/shard_map/ppermute | solution.py:337
  53.6 1.0 %collective-permute-start.3 = (bf16[16,16,256]{2,1,0:T(8,128)(2,1)S(1)}, bf16[16,16,256]{2,1,0:T(8,128)(2,1)S(1)}, u32[]{:S(2)}, u32[]{:S(2)}) collective-permute-start(bf16[16,16,256]{2,1,0:T(8,128)(2,1)S(1)} %join.18), channel_id=1, source_target_pairs={{0,2},{1,3},{2,0},{3,1},{4,6},{5,7},{6,4},{7,5},{8,10},{9,11},{10,... | collective-permute-start | bytes 393224 | tf_op jit(solution)/shard_map/ppermute | solution.py:337
  54.6 3.7 %collective-permute-done.5.refs_4_.refs_3_ = bf16[16,16,256]{2,1,0:T(8,128)(2,1)S(1)} collective-permute-done((bf16[16,16,256]{2,1,0:T(8,128)(2,1)S(1)}, bf16[16,16,256]{2,1,0:T(8,128)(2,1)S(1)}, u32[]{:S(2)}, u32[]{:S(2)}) %collective-permute-start.5) | collective-permute-done | bytes 131104 | tf_op jit(solution)/shard_map/ppermute | solution.py:337
  58.3 4.3 %collective-permute-done.4.refs_3_.refs_2_ = bf16[16,16,256]{2,1,0:T(8,128)(2,1)S(1)} collective-permute-done((bf16[16,16,256]{2,1,0:T(8,128)(2,1)S(1)}, bf16[16,16,256]{2,1,0:T(8,128)(2,1)S(1)}, u32[]{:S(2)}, u32[]{:S(2)}) %collective-permute-start.4) | collective-permute-done | bytes 131104 | tf_op jit(solution)/shard_map/ppermute | solution.py:337
  62.6 0.0 collective-permute-done.3.refs_2_.refs_1_
  62.6 0.0 collective-permute-done.16.refs_0_.refs_10_.refs_8_
  62.7 1.6 %collective-permute-start.17 = (bf16[72,16,256]{2,1,0:T(8,128)(2,1)S(1)}, bf16[72,16,256]{2,1,0:T(8,128)(2,1)S(1)}, u32[]{:S(2)}, u32[]{:S(2)}) collective-permute-start(bf16[72,16,256]{2,1,0:T(8,128)(2,1)S(1)} %join.33), channel_id=1, source_target_pairs={{8,0},{24,8},{16,24},{0,16},{9,1},{25,9},{17,25},{1,17},{10,2},{26... | collective-permute-start | bytes 1769480 | tf_op jit(solution)/shard_map/ppermute | solution.py:300
  64.2 0.0 collective-permute-done.12.refs_0_.refs_9_.refs_6_
  64.3 0.6 collective-permute-start.13
  64.8 0.9 turn.5.left_ref
  65.7 0.9 turn.4.left_ref
  66.6 0.9 turn.3.left_ref
  67.5 7.9 %stack.3.refs_13_ = bf16[48,2,256,1024]{3,2,1,0:T(8,128)(2,1)} custom-call(bf16[8,2,2,256,128]{4,3,2,1,0:T(8,128)(2,1)S(1)} %turn.5.left_ref, bf16[96,16,256]{2,1,0:T(8,128)(2,1)S(1)} %get-tuple-element.13.refs_0_, bf16[96,16,256]{2,1,0:T(8,128)(2,1)S(1)} %collective-permute-done.refs_1_, bf16[16,16,256]{2,1,0:T(8,128)(2,1)S(1)} %collective-permute-done.1.refs_1_.refs_2_, ...), custom_call_target="tpu_custom_call" | custom-call | flops 2147483648 | bytes 16777216 | tf_op jit(solution)/shard_map/stack/pallas_call | solution.py:259
  75.4 0.0 collective-permute-done.17.refs_0_.refs_12_.refs_8_
  75.4 1.6 %collective-permute-start.19 = (bf16[24,16,256]{2,1,0:T(8,128)(2,1)S(1)}, bf16[24,16,256]{2,1,0:T(8,128)(2,1)S(1)}, u32[]{:S(2)}, u32[]{:S(2)}) collective-permute-start(bf16[24,16,256]{2,1,0:T(8,128)(2,1)S(1)} %join.35), channel_id=1, source_target_pairs={{8,0},{24,8},{16,24},{0,16},{9,1},{25,9},{17,25},{1,17},{10,2},{26... | collective-permute-start | bytes 589832 | tf_op jit(solution)/shard_map/ppermute | solution.py:300
  77.0 0.0 collective-permute-done.13.refs_0_.refs_11_.refs_6_
  77.0 0.6 collective-permute-start.18
  77.6 7.9 %stack.4.refs_13_ = bf16[48,2,256,1024]{3,2,1,0:T(8,128)(2,1)} custom-call(bf16[8,2,2,256,128]{4,3,2,1,0:T(8,128)(2,1)S(1)} %turn.4.left_ref, bf16[96,16,256]{2,1,0:T(8,128)(2,1)S(1)} %get-tuple-element.13.refs_0_, bf16[96,16,256]{2,1,0:T(8,128)(2,1)S(1)} %collective-permute-done.refs_1_, ...), custom_call_target="tpu_custom_call", output_to_operand_aliasing={{}: (14, {})} | custom-call | flops 2147483648 | bytes 16777216 | tf_op jit(solution)/shard_map/stack/pallas_call | solution.py:259
  85.4 0.0 collective-permute-done.19.refs_12_
  85.4 0.0 collective-permute-done.18.refs_11_
  85.4 7.9 %stack.5 = bf16[48,2,256,1024]{3,2,1,0:T(8,128)(2,1)} custom-call(bf16[8,2,2,256,128]{4,3,2,1,0:T(8,128)(2,1)S(1)} %turn.3.left_ref, bf16[96,16,256]{2,1,0:T(8,128)(2,1)S(1)} %get-tuple-element.13.refs_0_, bf16[96,16,256]{2,1,0:T(8,128)(2,1)S(1)} %collective-permute-done.refs_1_, ...), custom_call_target="tpu_custom_call", output_to_operand_aliasing={{}: (14, {})} | custom-call | flops 2147483648 | bytes 16777216 | tf_op jit(solution)/shard_map/stack/pallas_call | solution.py:259
  (18 shorter events, 0.4 us)
Async XLA Ops:
  0.0 0.7 copy-start
  0.7 0.7 copy-start.1
  12.2 2.4 %collective-permute-start = (bf16[96,16,256]{2,1,0:T(8,128)(2,1)S(1)}, bf16[96,16,256]{2,1,0:T(8,128)(2,1)S(1)}, u32[]{:S(2)}, u32[]{:S(2)}) collective-permute-start(bf16[96,16,256]{2,1,0:T(8,128)(2,1)S(1)} %get-tuple-element.14), channel_id=1, source_target_pairs={{0,1},{1,0},{2,3},{3,2},{4,5},{5,4},{6,7},{7,6},{8,9},{9,8},{10,11... | collective-permute-start | bytes 2359304 | tf_op jit(solution)/shard_map/ppermute | solution.py:329
  14.6 17.8 %collective-permute-start.14 = (bf16[48,16,256]{2,1,0:T(8,128)(2,1)S(1)}, bf16[48,16,256]{2,1,0:T(8,128)(2,1)S(1)}, u32[]{:S(2)}, u32[]{:S(2)}) collective-permute-start(bf16[48,16,256]{2,1,0:T(8,128)(2,1)S(1)} %join.23), channel_id=1, source_target_pairs={{8,0},{24,8},{16,24},{0,16},{9,1},{25,9},{17,25},{1,17},{10,2},{26... | collective-permute-start | bytes 1179656 | tf_op jit(solution)/shard_map/ppermute | solution.py:300
  17.6 16.5 %collective-permute-start.6 = (bf16[48,16,256]{2,1,0:T(8,128)(2,1)S(1)}, bf16[48,16,256]{2,1,0:T(8,128)(2,1)S(1)}, u32[]{:S(2)}, u32[]{:S(2)}) collective-permute-start(bf16[48,16,256]{2,1,0:T(8,128)(2,1)S(1)} %join.23), channel_id=1, source_target_pairs={{0,8},{8,24},{24,16},{16,0},{1,9},{9,25},{25,17},{17,1},{2,10},{10... | collective-permute-start | bytes 1179656 | tf_op jit(solution)/shard_map/ppermute | solution.py:300
  17.6 6.7 %collective-permute-start.1 = (bf16[16,16,256]{2,1,0:T(8,128)(2,1)S(1)}, bf16[16,16,256]{2,1,0:T(8,128)(2,1)S(1)}, u32[]{:S(2)}, u32[]{:S(2)}) collective-permute-start(bf16[16,16,256]{2,1,0:T(8,128)(2,1)S(1)} %join.20), channel_id=1, source_target_pairs={{0,2},{1,3},{2,0},{3,1},{4,6},{5,7},{6,4},{7,5},{8,10},{9,11},{10,... | collective-permute-start | bytes 393224 | tf_op jit(solution)/shard_map/ppermute | solution.py:337
  19.7 12.7 %collective-permute-start.7 = (bf16[16,16,256]{2,1,0:T(8,128)(2,1)S(1)}, bf16[16,16,256]{2,1,0:T(8,128)(2,1)S(1)}, u32[]{:S(2)}, u32[]{:S(2)}) collective-permute-start(bf16[16,16,256]{2,1,0:T(8,128)(2,1)S(1)} %join.24), channel_id=1, source_target_pairs={{0,4},{1,5},{2,6},{3,7},{4,0},{5,1},{6,2},{7,3},{8,12},{9,13},{10,... | collective-permute-start | bytes 393224 | tf_op jit(solution)/shard_map/ppermute | solution.py:337
  22.4 10.1 %collective-permute-start.8 = (bf16[16,16,256]{2,1,0:T(8,128)(2,1)S(1)}, bf16[16,16,256]{2,1,0:T(8,128)(2,1)S(1)}, u32[]{:S(2)}, u32[]{:S(2)}) collective-permute-start(bf16[16,16,256]{2,1,0:T(8,128)(2,1)S(1)} %join.25), channel_id=1, source_target_pairs={{0,6},{1,7},{2,4},{3,5},{4,2},{5,3},{6,0},{7,1},{8,14},{9,15},{10,... | collective-permute-start | bytes 393224 | tf_op jit(solution)/shard_map/ppermute | solution.py:337
  32.5 15.3 %collective-permute-start.15 = (bf16[72,16,256]{2,1,0:T(8,128)(2,1)S(1)}, bf16[72,16,256]{2,1,0:T(8,128)(2,1)S(1)}, u32[]{:S(2)}, u32[]{:S(2)}) collective-permute-start(bf16[72,16,256]{2,1,0:T(8,128)(2,1)S(1)} %join.31), channel_id=1, source_target_pairs={{8,0},{24,8},{16,24},{0,16},{9,1},{25,9},{17,25},{1,17},{10,2},{26... | collective-permute-start | bytes 1769480 | tf_op jit(solution)/shard_map/ppermute | solution.py:300
  34.1 15.3 %collective-permute-start.9 = (bf16[72,16,256]{2,1,0:T(8,128)(2,1)S(1)}, bf16[72,16,256]{2,1,0:T(8,128)(2,1)S(1)}, u32[]{:S(2)}, u32[]{:S(2)}) collective-permute-start(bf16[72,16,256]{2,1,0:T(8,128)(2,1)S(1)} %join.26), channel_id=1, source_target_pairs={{0,8},{8,24},{24,16},{16,0},{1,9},{9,25},{25,17},{17,1},{2,10},{10... | collective-permute-start | bytes 1769480 | tf_op jit(solution)/shard_map/ppermute | solution.py:300
  34.7 5.9 %collective-permute-start.2 = (bf16[16,16,256]{2,1,0:T(8,128)(2,1)S(1)}, bf16[16,16,256]{2,1,0:T(8,128)(2,1)S(1)}, u32[]{:S(2)}, u32[]{:S(2)}) collective-permute-start(bf16[16,16,256]{2,1,0:T(8,128)(2,1)S(1)} %join.19), channel_id=1, source_target_pairs={{0,2},{1,3},{2,0},{3,1},{4,6},{5,7},{6,4},{7,5},{8,10},{9,11},{10,... | collective-permute-start | bytes 393224 | tf_op jit(solution)/shard_map/ppermute | solution.py:337
  36.8 11.1 %collective-permute-start.10 = (bf16[16,16,256]{2,1,0:T(8,128)(2,1)S(1)}, bf16[16,16,256]{2,1,0:T(8,128)(2,1)S(1)}, u32[]{:S(2)}, u32[]{:S(2)}) collective-permute-start(bf16[16,16,256]{2,1,0:T(8,128)(2,1)S(1)} %join.27), channel_id=1, source_target_pairs={{0,4},{1,5},{2,6},{3,7},{4,0},{5,1},{6,2},{7,3},{8,12},{9,13},{10,... | collective-permute-start | bytes 393224 | tf_op jit(solution)/shard_map/ppermute | solution.py:337
  37.8 10.0 %collective-permute-start.11 = (bf16[16,16,256]{2,1,0:T(8,128)(2,1)S(1)}, bf16[16,16,256]{2,1,0:T(8,128)(2,1)S(1)}, u32[]{:S(2)}, u32[]{:S(2)}) collective-permute-start(bf16[16,16,256]{2,1,0:T(8,128)(2,1)S(1)} %join.28), channel_id=1, source_target_pairs={{0,6},{1,7},{2,4},{3,5},{4,2},{5,3},{6,0},{7,1},{8,14},{9,15},{10,... | collective-permute-start | bytes 393224 | tf_op jit(solution)/shard_map/ppermute | solution.py:337
  47.9 14.7 %collective-permute-start.16 = (bf16[72,16,256]{2,1,0:T(8,128)(2,1)S(1)}, bf16[72,16,256]{2,1,0:T(8,128)(2,1)S(1)}, u32[]{:S(2)}, u32[]{:S(2)}) collective-permute-start(bf16[72,16,256]{2,1,0:T(8,128)(2,1)S(1)} %join.32), channel_id=1, source_target_pairs={{8,0},{24,8},{16,24},{0,16},{9,1},{25,9},{17,25},{1,17},{10,2},{26... | collective-permute-start | bytes 1769480 | tf_op jit(solution)/shard_map/ppermute | solution.py:300
  49.5 14.7 %collective-permute-start.12 = (bf16[72,16,256]{2,1,0:T(8,128)(2,1)S(1)}, bf16[72,16,256]{2,1,0:T(8,128)(2,1)S(1)}, u32[]{:S(2)}, u32[]{:S(2)}) collective-permute-start(bf16[72,16,256]{2,1,0:T(8,128)(2,1)S(1)} %join.29), channel_id=1, source_target_pairs={{0,8},{8,24},{24,16},{16,0},{1,9},{9,25},{25,17},{17,1},{2,10},{10... | collective-permute-start | bytes 1769480 | tf_op jit(solution)/shard_map/ppermute | solution.py:300
  50.1 8.2 %collective-permute-start.5 = (bf16[16,16,256]{2,1,0:T(8,128)(2,1)S(1)}, bf16[16,16,256]{2,1,0:T(8,128)(2,1)S(1)}, u32[]{:S(2)}, u32[]{:S(2)}) collective-permute-start(bf16[16,16,256]{2,1,0:T(8,128)(2,1)S(1)} %join.22), channel_id=1, source_target_pairs={{0,6},{1,7},{2,4},{3,5},{4,2},{5,3},{6,0},{7,1},{8,14},{9,15},{10,... | collective-permute-start | bytes 393224 | tf_op jit(solution)/shard_map/ppermute | solution.py:337
  52.0 10.6 %collective-permute-start.4 = (bf16[16,16,256]{2,1,0:T(8,128)(2,1)S(1)}, bf16[16,16,256]{2,1,0:T(8,128)(2,1)S(1)}, u32[]{:S(2)}, u32[]{:S(2)}) collective-permute-start(bf16[16,16,256]{2,1,0:T(8,128)(2,1)S(1)} %join.21), channel_id=1, source_target_pairs={{0,4},{1,5},{2,6},{3,7},{4,0},{5,1},{6,2},{7,3},{8,12},{9,13},{10,... | collective-permute-start | bytes 393224 | tf_op jit(solution)/shard_map/ppermute | solution.py:337
  53.6 9.0 %collective-permute-start.3 = (bf16[16,16,256]{2,1,0:T(8,128)(2,1)S(1)}, bf16[16,16,256]{2,1,0:T(8,128)(2,1)S(1)}, u32[]{:S(2)}, u32[]{:S(2)}) collective-permute-start(bf16[16,16,256]{2,1,0:T(8,128)(2,1)S(1)} %join.18), channel_id=1, source_target_pairs={{0,2},{1,3},{2,0},{3,1},{4,6},{5,7},{6,4},{7,5},{8,10},{9,11},{10,... | collective-permute-start | bytes 393224 | tf_op jit(solution)/shard_map/ppermute | solution.py:337
  62.7 12.7 %collective-permute-start.17 = (bf16[72,16,256]{2,1,0:T(8,128)(2,1)S(1)}, bf16[72,16,256]{2,1,0:T(8,128)(2,1)S(1)}, u32[]{:S(2)}, u32[]{:S(2)}) collective-permute-start(bf16[72,16,256]{2,1,0:T(8,128)(2,1)S(1)} %join.33), channel_id=1, source_target_pairs={{8,0},{24,8},{16,24},{0,16},{9,1},{25,9},{17,25},{1,17},{10,2},{26... | collective-permute-start | bytes 1769480 | tf_op jit(solution)/shard_map/ppermute | solution.py:300
  64.3 12.7 %collective-permute-start.13 = (bf16[72,16,256]{2,1,0:T(8,128)(2,1)S(1)}, bf16[72,16,256]{2,1,0:T(8,128)(2,1)S(1)}, u32[]{:S(2)}, u32[]{:S(2)}) collective-permute-start(bf16[72,16,256]{2,1,0:T(8,128)(2,1)S(1)} %join.30), channel_id=1, source_target_pairs={{0,8},{8,24},{24,16},{16,0},{1,9},{9,25},{25,17},{17,1},{2,10},{10... | collective-permute-start | bytes 1769480 | tf_op jit(solution)/shard_map/ppermute | solution.py:300
  75.4 10.0 %collective-permute-start.19 = (bf16[24,16,256]{2,1,0:T(8,128)(2,1)S(1)}, bf16[24,16,256]{2,1,0:T(8,128)(2,1)S(1)}, u32[]{:S(2)}, u32[]{:S(2)}) collective-permute-start(bf16[24,16,256]{2,1,0:T(8,128)(2,1)S(1)} %join.35), channel_id=1, source_target_pairs={{8,0},{24,8},{16,24},{0,16},{9,1},{25,9},{17,25},{1,17},{10,2},{26... | collective-permute-start | bytes 589832 | tf_op jit(solution)/shard_map/ppermute | solution.py:300
  77.0 8.5 %collective-permute-start.18 = (bf16[24,16,256]{2,1,0:T(8,128)(2,1)S(1)}, bf16[24,16,256]{2,1,0:T(8,128)(2,1)S(1)}, u32[]{:S(2)}, u32[]{:S(2)}) collective-permute-start(bf16[24,16,256]{2,1,0:T(8,128)(2,1)S(1)} %join.34), channel_id=1, source_target_pairs={{0,8},{8,24},{24,16},{16,0},{1,9},{9,25},{25,17},{17,1},{2,10},{10... | collective-permute-start | bytes 589832 | tf_op jit(solution)/shard_map/ppermute | solution.py:300
